TPU v7x, 32 devices: a whole 2x2x4 slice. The times are simulated.
32 devices in a mesh: blk: 16 (over z, y, x), rep: 2 (over core).
Axes of the slice: x: 2, y: 2, z: 4, core: 2. Of those that a mesh axis runs over, the one named last changes fastest.
Arguments:
- points: float32 [64, 16384], P(None, 'blk'), may hold values from -1 to 1
- lengthscale: float32 [64], replicated, may hold values from 0.5 to 2
- noise: float32 [16384], P('blk'), may hold values from 0.5 to 2
- target: float32 [16, 16384], P(None, 'blk'), may hold values from -20 to 20
- pair_offset: int32 [16, 8], P('blk'), may hold values from 1 to 8, as said below
- pair_count: int32 [16], P('blk'), may hold values from 0 to 8
Outputs:
- solution: float32 [16, 16384], P(None, 'blk')
- residual: float32 [16, 16384], P(None, 'blk')
Inputs may be any that keep to these rules, and one draw needn't show every extreme that they name: `pair_offset`: in row b the first pair_count[b] entries are distinct and b plus each of them is below 16; the other entries are unused.
All inputs are finite; a program needn't handle non-finite values.
Results may differ from a plain program's by a relative error of at most 0.0003.
Values may be sent and summed in bfloat16 or wider, within the bound.
A program may use at most 64 MiB of HBM per device.

v0:
```python
import jax
import jax.numpy as jnp
from jax import lax
from jax.sharding import PartitionSpec as P

B = 1024
W = 8
ITERS = 2


exact = lax.Precision.HIGHEST


def from_behind(value, axis, steps):
    count = lax.axis_size(axis)
    initial, last = (max(0, -steps), min(count, count - steps))
    return lax.ppermute(value, axis, [(source, source + steps) for source in range(initial, last)])


def kernel_tile(rows_z, cols_z):
    inner_prod = lax.dot_general(
        rows_z,
        cols_z,
        (((0,), (0,)), ((), ())),
        precision=exact,
        preferred_element_type=jnp.float32,
    )
    square = (
        jnp.sum(rows_z * rows_z, axis=0)[:, None]
        + jnp.sum(cols_z * cols_z, axis=0)[None, :]
        - 2.0 * inner_prod
    )
    radius = jnp.sqrt(jnp.maximum(square, 0.0))
    margin = jnp.maximum(1.0 - radius, 0.0)
    margin_sq = margin * margin
    return 1.0 / B * margin_sq * margin_sq * (4.0 * radius + 1.0)


def apply_tile(vectors, kernel_low):
    return lax.dot_general(
        vectors, kernel_low, (((1,), (1,)), ((), ())), preferred_element_type=jnp.float32
    )


def squares(residual):
    return lax.psum(jnp.sum(residual * residual, axis=1), "blk")


def body(points, lengthscale, noise, target, pair_offset, pair_count):
    scaled = points / lengthscale[:, None]
    block_rows = points.shape[1]
    core_index = lax.axis_index("rep")
    live_pairs = pair_count[0]
    offsets = pair_offset[0]
    middle = (live_pairs + 1) // 2
    slot_begin = jnp.where(core_index == 0, 0, middle)
    slot_end = jnp.where(core_index == 0, middle, live_pairs)
    diag_rows = block_rows // 2
    row_start = core_index * diag_rows
    solution = jnp.zeros_like(target)
    residual = target
    direction = target
    norm_now = squares(residual)
    for iteration in range(ITERS):
        rounded = direction.astype(jnp.bfloat16)
        fetched = [
            from_behind((scaled, direction), "blk", -distance) for distance in range(1, W + 1)
        ]
        partner_z = jnp.stack([received[0] for received in fetched])
        partner_v = jnp.stack([received[1] for received in fetched]).astype(jnp.bfloat16)
        row_z = lax.dynamic_slice_in_dim(scaled, row_start, diag_rows, 1)
        kernel = kernel_tile(row_z, scaled)
        own_prod = lax.dynamic_update_slice_in_dim(
            jnp.zeros(direction.shape, jnp.float32),
            apply_tile(rounded, kernel.astype(jnp.bfloat16)),
            row_start,
            1,
        )
        own_deg = lax.dynamic_update_slice_in_dim(
            jnp.zeros((block_rows,), jnp.float32), jnp.sum(kernel, axis=1), row_start, 0
        )

        def visit_pair(slot_id, state_now):
            own_prod, own_deg, sent_prod, sent_deg = state_now
            slot_index = offsets[slot_id] - 1
            kernel = kernel_tile(scaled, partner_z[slot_index])
            kernel_low = kernel.astype(jnp.bfloat16)
            own_prod = own_prod + apply_tile(partner_v[slot_index], kernel_low)
            own_deg = own_deg + jnp.sum(kernel, axis=1)
            toward = jnp.dot(rounded, kernel_low, preferred_element_type=jnp.float32)
            sent_prod = sent_prod.at[slot_index].add(toward)
            sent_deg = sent_deg.at[slot_index].add(jnp.sum(kernel, axis=0))
            return (own_prod, own_deg, sent_prod, sent_deg)

        initial = (
            own_prod,
            own_deg,
            jnp.zeros((W,) + direction.shape, jnp.float32),
            jnp.zeros((W, block_rows), jnp.float32),
        )
        own_prod, own_deg, sent_prod, sent_deg = lax.fori_loop(
            slot_begin, slot_end, visit_pair, initial
        )
        for distance in range(1, W + 1):
            back_prod, back_deg = from_behind(
                (sent_prod[distance - 1], sent_deg[distance - 1]), "blk", distance
            )
            own_prod = own_prod + back_prod
            own_deg = own_deg + back_deg
        own_prod, own_deg = lax.psum((own_prod, own_deg), "rep")
        applied = (noise + own_deg)[None, :] * direction + own_prod
        step_size = norm_now / lax.psum(jnp.sum(direction * applied, axis=1), "blk")
        solution = solution + step_size[:, None] * direction
        residual = residual - step_size[:, None] * applied
        if iteration + 1 < ITERS:
            norm_next = squares(residual)
            direction = residual + (norm_next / norm_now)[:, None] * direction
            norm_now = norm_next
    return (solution, residual)


def solution(mesh):
    placed = (P(None, "blk"), P(), P("blk"), P(None, "blk"), P("blk", None), P("blk"))
    return jax.shard_map(
        body,
        mesh=mesh,
        in_specs=placed,
        out_specs=(P(None, "blk"), P(None, "blk")),
        check_vma=False,
    )
```

profile of v0, /device:TPU:0, one launch (start us, length us, event | category | flops | bytes accessed | tf_op | source)
XLA Modules:
  0.0 509.4 jit_solution(13887668951994193502)
XLA Ops:
  7.2 1.7 multiply_reduce_fusion
  10.2 1.3 collective-permute-start.9
  11.5 1.3 collective-permute-start.10
  12.8 1.3 collective-permute-start.11
  17.2 4.3 fusion.43
  24.1 8.8 %collective-permute-done.1 = bf16[16,1024]{1,0:T(8,128)(2,1)S(1)} collective-permute-done((bf16[16,1024]{1,0:T(8,128)(2,1)S(1)}, bf16[16,1024]{1,0:T(8,128)(2,1)S(1)}, u32[]{:S(2)}, u32[]{:S(2)}) %collective-permute-start.1) | collective-permute-done | bytes 32800 | tf_op jit(solution)/shard_map/ppermute | solution.py:17
  34.2 19.7 %collective-permute-done.2 = bf16[16,1024]{1,0:T(8,128)(2,1)S(1)} collective-permute-done((bf16[16,1024]{1,0:T(8,128)(2,1)S(1)}, bf16[16,1024]{1,0:T(8,128)(2,1)S(1)}, u32[]{:S(2)}, u32[]{:S(2)}) %collective-permute-start.2) | collective-permute-done | bytes 32800 | tf_op jit(solution)/shard_map/ppermute | solution.py:17
  55.2 4.5 collective-permute-done.3
  61.0 5.4 %collective-permute-done.4 = bf16[16,1024]{1,0:T(8,128)(2,1)S(1)} collective-permute-done((bf16[16,1024]{1,0:T(8,128)(2,1)S(1)}, bf16[16,1024]{1,0:T(8,128)(2,1)S(1)}, u32[]{:S(2)}, u32[]{:S(2)}) %collective-permute-start.4) | collective-permute-done | bytes 32800 | tf_op jit(solution)/shard_map/ppermute | solution.py:17
  67.7 5.4 %collective-permute-done.5 = bf16[16,1024]{1,0:T(8,128)(2,1)S(1)} collective-permute-done((bf16[16,1024]{1,0:T(8,128)(2,1)S(1)}, bf16[16,1024]{1,0:T(8,128)(2,1)S(1)}, u32[]{:S(2)}, u32[]{:S(2)}) %collective-permute-start.5) | collective-permute-done | bytes 32800 | tf_op jit(solution)/shard_map/ppermute | solution.py:17
  74.4 9.3 %collective-permute-done.6 = bf16[16,1024]{1,0:T(8,128)(2,1)S(1)} collective-permute-done((bf16[16,1024]{1,0:T(8,128)(2,1)S(1)}, bf16[16,1024]{1,0:T(8,128)(2,1)S(1)}, u32[]{:S(2)}, u32[]{:S(2)}) %collective-permute-start.6) | collective-permute-done | bytes 32800 | tf_op jit(solution)/shard_map/ppermute | solution.py:17
  85.0 22.3 %collective-permute-done.7 = bf16[16,1024]{1,0:T(8,128)(2,1)S(1)} collective-permute-done((bf16[16,1024]{1,0:T(8,128)(2,1)S(1)}, bf16[16,1024]{1,0:T(8,128)(2,1)S(1)}, u32[]{:S(2)}, u32[]{:S(2)}) %collective-permute-start.7) | collective-permute-done | bytes 32800 | tf_op jit(solution)/shard_map/ppermute | solution.py:17
  112.4 1.3 collective-permute-start.14
  114.7 1.3 collective-permute-start.15
  119.5 3.2 collective-permute-done.14
  122.7 11.3 %collective-permute-done.15 = f32[64,1024]{1,0:T(8,128)S(1)} collective-permute-done((f32[64,1024]{1,0:T(8,128)}, f32[64,1024]{1,0:T(8,128)S(1)}, u32[]{:S(2)}, u32[]{:S(2)}) %collective-permute-start.15) | collective-permute-done | bytes 262176 | tf_op jit(solution)/shard_map/ppermute | solution.py:17
  134.9 15.7 %while.44 = (s32[]{:T(128)}, f32[16,1024]{1,0:T(8,128)S(1)}, f32[1024]{0:T(1024)S(1)}, f32[8,16,1024]{2,1,0:T(8,128)}, f32[8,1024]{1,0:T(8,128)S(1)}, /*index=5*...) while((s32[]{:T(128)}, f32[16,1024]{1,0:T(8,128)S(1)}, ...), condition=%wide.region_11.12_spmd, body=%wide.region_5.11_spmd.sunk | while | flops 888324096 | bytes 7460680 | solution.py:101
  137.0 7.6 %fusion.79 = (f32[1024]{0:T(1024)S(1)}, f32[1024]{0:T(1024)S(1)}, bf16[1024,1024]{0,1:T(8,128)(2,1)S(1)}) fusion(f32[64,1024]{1,0:T(8,128)} %get-tuple-element.869, f32[8,64,1024]{2,1,0:T(8,128)S(1)} %get-tuple-element.868, s32[]{:T(128)} %select_n.75, f32[1024]{0:T(1024)S(1)} %fusion.78, f32[1024]{0:T(1024)S(1)} %get-tuple-element.867), kind=kOutput, calls=%fused_computation.112.clone.1 | convolution fusion | flops 821032960 | bytes 2637828 | tf_op jit(solution)/shard_map/while/body/dot_general | solution.py:21
  145.4 2.7 fusion.80
  151.8 1.3 collective-permute-start.24
  153.1 39.1 %collective-permute-start.25 = (f32[16,1024]{1,0:T(8,128)S(1)}, f32[16,1024]{1,0:T(8,128)S(1)}, u32[]{:S(2)}, u32[]{:S(2)}) collective-permute-start(f32[16,1024]{1,0:T(8,128)S(1)} %get-tuple-element.613), channel_id=1, source_target_pairs={{0,4},{2,6},{4,8},{6,10},{8,12},{10,14},{12,16},{14,18},{16,20},{1... | collective-permute-start | bytes 196616 | tf_op jit(solution)/shard_map/ppermute | solution.py:17
  192.2 9.1 %collective-permute-start.26 = (f32[16,1024]{1,0:T(8,128)S(1)}, f32[16,1024]{1,0:T(8,128)S(1)}, u32[]{:S(2)}, u32[]{:S(2)}) collective-permute-start(f32[16,1024]{1,0:T(8,128)S(1)} %get-tuple-element.612), channel_id=1, source_target_pairs={{0,6},{2,8},{4,10},{6,12},{8,14},{10,16},{12,18},{14,20},{16,22},{... | collective-permute-start | bytes 196616 | tf_op jit(solution)/shard_map/ppermute | solution.py:17
  201.3 2.5 collective-permute-start.16
  203.7 1.9 collective-permute-start.17
  205.7 3.0 collective-permute-start.18
  208.7 2.8 collective-permute-start.27
  211.5 3.3 collective-permute-start.28
  214.8 1.3 collective-permute-start.29
  216.1 3.2 collective-permute-start.30
  219.3 1.3 collective-permute-start.31
  220.6 1.3 collective-permute-start.19
  224.6 4.4 collective-permute-start.22
  231.6 2.5 psum.57
  234.1 10.6 %all-reduce.4.cloned.1.call-done = f32[16,1024]{1,0:T(8,128)} async-done(((f32[16,1024]{1,0:T(8,128)}), f32[16,1024]{1,0:T(8,128)}) %all-reduce.4.cloned.1.call-update) | async-done | bytes 65552 | tf_op jit(solution)/shard_map/psum | solution.py:110
  245.7 42.0 %all-reduce = (f32[16]{0:T(128)S(1)}, f32[16]{0:T(128)S(1)}) all-reduce(f32[16]{0:T(128)S(1)} %get-tuple-element.541, f32[16]{0:T(128)S(1)} %get-tuple-element.540), channel_id=1, replica_groups=mesh['blk'=16,'rep'=2] {'blk'}, use_global_device_ids=true, to_apply=%region_1.2 | all-reduce | flops 32 | bytes 256 | tf_op jit(solution)/shard_map/psum | solution.py:46
  288.7 36.6 %psum.60 = f32[16]{0:T(128)S(1)} all-reduce(f32[16]{0:T(128)S(1)} %multiply_reduce_fusion.3), channel_id=1, replica_groups=mesh['blk'=16,'rep'=2] {'blk'}, use_global_device_ids=true, to_apply=%region_17.18 | all-reduce | flops 16 | bytes 128 | tf_op jit(solution)/shard_map/psum | solution.py:46
  326.2 1.3 collective-permute-start.32
  327.5 1.3 collective-permute-start.33
  328.8 1.3 collective-permute-start.34
  330.1 1.3 collective-permute-start.35
  331.4 1.3 collective-permute-start.36
  333.1 1.3 collective-permute-start.37
  338.6 2.1 collective-permute-done.35
  340.7 2.8 collective-permute-done.36
  343.5 1.4 collective-permute-done.37
  344.9 4.3 collective-permute-done.38
  349.7 13.7 %while.45 = (s32[]{:T(128)}, f32[16,1024]{1,0:T(8,128)S(1)}, f32[1024]{0:T(1024)S(1)}, f32[8,16,1024]{2,1,0:T(8,128)S(1)}, f32[8,1024]{1,0:T(8,128)S(1)}, /*inde...) while((s32[]{:T(128)}, f32[16,1024]{1,0:T(8,128)S(1)}, ...), condition=%wide.region_24.25_spmd, body=%wide.region_18.24_spmd.sunk | while | flops 888324096 | bytes 7459153 | solution.py:101
  351.9 7.6 %fusion.87 = (f32[1024]{0:T(1024)S(1)}, f32[1024]{0:T(1024)S(1)}, bf16[1024,1024]{0,1:T(8,128)(2,1)S(1)}) fusion(f32[64,1024]{1,0:T(8,128)} %get-tuple-element.929, f32[8,64,1024]{2,1,0:T(8,128)S(1)} %get-tuple-element.928, s32[]{:T(128)} %select_n.77, f32[1024]{0:T(1024)S(1)} %fusion.86, f32[1024]{0:T(1024)S(1)} %get-tuple-element.927), kind=kOutput, calls=%fused_computation.113.clone.1 | convolution fusion | flops 821032960 | bytes 2637828 | tf_op jit(solution)/shard_map/while/body/dot_general | solution.py:21
  363.5 2.8 collective-permute-start.48
  366.3 42.7 %collective-permute-start.49 = (f32[16,1024]{1,0:T(8,128)S(1)}, f32[16,1024]{1,0:T(8,128)S(1)}, u32[]{:S(2)}, u32[]{:S(2)}) collective-permute-start(f32[16,1024]{1,0:T(8,128)S(1)} %get-tuple-element.605), channel_id=1, source_target_pairs={{0,4},{2,6},{4,8},{6,10},{8,12},{10,14},{12,16},{14,18},{16,20},{1... | collective-permute-start | bytes 196616 | tf_op jit(solution)/shard_map/ppermute | solution.py:17
  409.1 5.5 %collective-permute-start.50 = (f32[16,1024]{1,0:T(8,128)S(1)}, f32[16,1024]{1,0:T(8,128)S(1)}, u32[]{:S(2)}, u32[]{:S(2)}) collective-permute-start(f32[16,1024]{1,0:T(8,128)S(1)} %get-tuple-element.604), channel_id=1, source_target_pairs={{0,6},{2,8},{4,10},{6,12},{8,14},{10,16},{12,18},{14,20},{16,22},{... | collective-permute-start | bytes 196616 | tf_op jit(solution)/shard_map/ppermute | solution.py:17
  414.6 2.5 collective-permute-start.40
  417.1 1.9 collective-permute-start.41
  419.0 3.0 collective-permute-start.42
  422.0 2.8 collective-permute-start.51
  424.9 3.3 collective-permute-start.52
  428.1 1.3 collective-permute-start.53
  429.4 3.2 collective-permute-start.54
  432.6 1.3 collective-permute-start.55
  437.9 4.4 collective-permute-start.46
  444.9 2.5 psum.61
  447.4 10.6 %all-reduce.6.cloned.1.call-done = f32[16,1024]{1,0:T(8,128)} async-done(((f32[16,1024]{1,0:T(8,128)}), f32[16,1024]{1,0:T(8,128)}) %all-reduce.6.cloned.1.call-update) | async-done | bytes 65552 | tf_op jit(solution)/shard_map/psum | solution.py:110
  459.0 42.0 %psum.63 = f32[16]{0:T(128)S(1)} all-reduce(f32[16]{0:T(128)S(1)} %multiply_reduce_fusion.2), channel_id=1, replica_groups=mesh['blk'=16,'rep'=2] {'blk'}, use_global_device_ids=true, to_apply=%region_28.29 | all-reduce | flops 16 | bytes 128 | tf_op jit(solution)/shard_map/psum | solution.py:112
  501.0 1.6 multiply_subtract_fusion
  (155 shorter events, 54.6 us)
Async XLA Ops:
  7.2 237.5 %all-reduce.4.cloned.1.call-start = ((), (), s32[]{:S(2)}) async-start(), calls=%async_computation | async-start | bytes 131072 | tf_op jit(solution)/shard_map/psum | solution.py:110
  9.0 99.7 %collective-permute-start.8 = (f32[64,1024]{1,0:T(8,128)}, f32[64,1024]{1,0:T(8,128)S(1)}, u32[]{:S(2)}, u32[]{:S(2)}) collective-permute-start(f32[64,1024]{1,0:T(8,128)} %get-tuple-element.889), channel_id=1, source_target_pairs={{2,0},{4,2},{6,4},{8,6},{10,8},{12,10},{14,12},{16,14},{18,16},{20... | collective-permute-start | bytes 786440 | tf_op jit(solution)/shard_map/ppermute | solution.py:17
  10.2 102.2 %collective-permute-start.9 = (f32[64,1024]{1,0:T(8,128)}, f32[64,1024]{1,0:T(8,128)}, u32[]{:S(2)}, u32[]{:S(2)}) collective-permute-start(f32[64,1024]{1,0:T(8,128)} %get-tuple-element.889), channel_id=1, source_target_pairs={{4,0},{6,2},{8,4},{10,6},{12,8},{14,10},{16,12},{18,14},{20,16},{2... | collective-permute-start | bytes 786440 | tf_op jit(solution)/shard_map/ppermute | solution.py:17
  11.5 103.1 %collective-permute-start.10 = (f32[64,1024]{1,0:T(8,128)}, f32[64,1024]{1,0:T(8,128)}, u32[]{:S(2)}, u32[]{:S(2)}) collective-permute-start(f32[64,1024]{1,0:T(8,128)} %get-tuple-element.889), channel_id=1, source_target_pairs={{6,0},{8,2},{10,4},{12,6},{14,8},{16,10},{18,12},{20,14},{22,16},{... | collective-permute-start | bytes 786440 | tf_op jit(solution)/shard_map/ppermute | solution.py:17
  12.8 104.1 %collective-permute-start.11 = (f32[64,1024]{1,0:T(8,128)}, f32[64,1024]{1,0:T(8,128)}, u32[]{:S(2)}, u32[]{:S(2)}) collective-permute-start(f32[64,1024]{1,0:T(8,128)} %get-tuple-element.889), channel_id=1, source_target_pairs={{8,0},{10,2},{12,4},{14,6},{16,8},{18,10},{20,12},{22,14},{24,16},... | collective-permute-start | bytes 786440 | tf_op jit(solution)/shard_map/ppermute | solution.py:17
  15.0 7.9 %collective-permute-start = (bf16[16,1024]{1,0:T(8,128)(2,1)S(1)}, bf16[16,1024]{1,0:T(8,128)(2,1)S(1)}, u32[]{:S(2)}, u32[]{:S(2)}) collective-permute-start(bf16[16,1024]{1,0:T(8,128)(2,1)S(1)} %convert.174), channel_id=1, source_target_pairs={{2,0},{4,2},{6,4},{8,6},{10,8},{12,10},{14,12},{16,14},{18,16},{20... | collective-permute-start | bytes 98312 | tf_op jit(solution)/shard_map/ppermute | solution.py:17
  22.8 10.1 %collective-permute-start.1 = (bf16[16,1024]{1,0:T(8,128)(2,1)S(1)}, bf16[16,1024]{1,0:T(8,128)(2,1)S(1)}, u32[]{:S(2)}, u32[]{:S(2)}) collective-permute-start(bf16[16,1024]{1,0:T(8,128)(2,1)S(1)} %convert.174), channel_id=1, source_target_pairs={{4,0},{6,2},{8,4},{10,6},{12,8},{14,10},{16,12},{18,14},{20,16},{2... | collective-permute-start | bytes 98312 | tf_op jit(solution)/shard_map/ppermute | solution.py:17
  32.9 21.0 %collective-permute-start.2 = (bf16[16,1024]{1,0:T(8,128)(2,1)S(1)}, bf16[16,1024]{1,0:T(8,128)(2,1)S(1)}, u32[]{:S(2)}, u32[]{:S(2)}) collective-permute-start(bf16[16,1024]{1,0:T(8,128)(2,1)S(1)} %convert.174), channel_id=1, source_target_pairs={{6,0},{8,2},{10,4},{12,6},{14,8},{16,10},{18,12},{20,14},{22,16},{... | collective-permute-start | bytes 98312 | tf_op jit(solution)/shard_map/ppermute | solution.py:17
  53.9 5.8 %collective-permute-start.3 = (bf16[16,1024]{1,0:T(8,128)(2,1)S(1)}, bf16[16,1024]{1,0:T(8,128)(2,1)S(1)}, u32[]{:S(2)}, u32[]{:S(2)}) collective-permute-start(bf16[16,1024]{1,0:T(8,128)(2,1)S(1)} %convert.174), channel_id=1, source_target_pairs={{8,0},{10,2},{12,4},{14,6},{16,8},{18,10},{20,12},{22,14},{24,16},... | collective-permute-start | bytes 98312 | tf_op jit(solution)/shard_map/ppermute | solution.py:17
  59.7 6.7 %collective-permute-start.4 = (bf16[16,1024]{1,0:T(8,128)(2,1)S(1)}, bf16[16,1024]{1,0:T(8,128)(2,1)S(1)}, u32[]{:S(2)}, u32[]{:S(2)}) collective-permute-start(bf16[16,1024]{1,0:T(8,128)(2,1)S(1)} %convert.174), channel_id=1, source_target_pairs={{10,0},{12,2},{14,4},{16,6},{18,8},{20,10},{22,12},{24,14},{26,16}... | collective-permute-start | bytes 98312 | tf_op jit(solution)/shard_map/ppermute | solution.py:17
  66.4 6.7 %collective-permute-start.5 = (bf16[16,1024]{1,0:T(8,128)(2,1)S(1)}, bf16[16,1024]{1,0:T(8,128)(2,1)S(1)}, u32[]{:S(2)}, u32[]{:S(2)}) collective-permute-start(bf16[16,1024]{1,0:T(8,128)(2,1)S(1)} %convert.174), channel_id=1, source_target_pairs={{12,0},{14,2},{16,4},{18,6},{20,8},{22,10},{24,12},{26,14},{28,16}... | collective-permute-start | bytes 98312 | tf_op jit(solution)/shard_map/ppermute | solution.py:17
  73.1 10.6 %collective-permute-start.6 = (bf16[16,1024]{1,0:T(8,128)(2,1)S(1)}, bf16[16,1024]{1,0:T(8,128)(2,1)S(1)}, u32[]{:S(2)}, u32[]{:S(2)}) collective-permute-start(bf16[16,1024]{1,0:T(8,128)(2,1)S(1)} %convert.174), channel_id=1, source_target_pairs={{14,0},{16,2},{18,4},{20,6},{22,8},{24,10},{26,12},{28,14},{30,16}... | collective-permute-start | bytes 98312 | tf_op jit(solution)/shard_map/ppermute | solution.py:17
  83.7 23.6 %collective-permute-start.7 = (bf16[16,1024]{1,0:T(8,128)(2,1)S(1)}, bf16[16,1024]{1,0:T(8,128)(2,1)S(1)}, u32[]{:S(2)}, u32[]{:S(2)}) collective-permute-start(bf16[16,1024]{1,0:T(8,128)(2,1)S(1)} %convert.174), channel_id=1, source_target_pairs={{16,0},{18,2},{20,4},{22,6},{24,8},{26,10},{28,12},{30,14},{17,1},... | collective-permute-start | bytes 98312 | tf_op jit(solution)/shard_map/ppermute | solution.py:17
  107.4 11.1 %collective-permute-start.12 = (f32[64,1024]{1,0:T(8,128)}, f32[64,1024]{1,0:T(8,128)S(1)}, u32[]{:S(2)}, u32[]{:S(2)}) collective-permute-start(f32[64,1024]{1,0:T(8,128)} %get-tuple-element.889), channel_id=1, source_target_pairs={{10,0},{12,2},{14,4},{16,6},{18,8},{20,10},{22,12},{24,14},{26,16}... | collective-permute-start | bytes 786440 | tf_op jit(solution)/shard_map/ppermute | solution.py:17
  110.1 9.4 %collective-permute-start.13 = (f32[64,1024]{1,0:T(8,128)}, f32[64,1024]{1,0:T(8,128)S(1)}, u32[]{:S(2)}, u32[]{:S(2)}) collective-permute-start(f32[64,1024]{1,0:T(8,128)} %get-tuple-element.889), channel_id=1, source_target_pairs={{12,0},{14,2},{16,4},{18,6},{20,8},{22,10},{24,12},{26,14},{28,16}... | collective-permute-start | bytes 786440 | tf_op jit(solution)/shard_map/ppermute | solution.py:17
  112.4 22.5 %copy-start.4 = (s32[3]{0:T(128)S(1)}, s32[3]{0:T(128)}, u32[]{:S(2)}) copy-start(s32[3]{0:T(128)} %constant.307.clone.1) | copy-start | bytes 40
  112.4 22.5 %copy-start.5 = (s32[2]{0:T(128)S(1)}, s32[2]{0:T(128)}, u32[]{:S(2)}) copy-start(s32[2]{0:T(128)} %constant.309.clone.1) | copy-start | bytes 28
  112.4 22.5 %copy-start.7 = (s32[1,8]{1,0:T(1,128)S(1)}, s32[1,8]{1,0:T(1,128)}, u32[]{:S(2)}) copy-start(s32[1,8]{1,0:T(1,128)} %param.22) | copy-start | bytes 100
  112.4 10.3 %collective-permute-start.14 = (f32[64,1024]{1,0:T(8,128)}, f32[64,1024]{1,0:T(8,128)S(1)}, u32[]{:S(2)}, u32[]{:S(2)}) collective-permute-start(f32[64,1024]{1,0:T(8,128)} %get-tuple-element.889), channel_id=1, source_target_pairs={{14,0},{16,2},{18,4},{20,6},{22,8},{24,10},{26,12},{28,14},{30,16}... | collective-permute-start | bytes 786440 | tf_op jit(solution)/shard_map/ppermute | solution.py:17
  114.7 19.3 %collective-permute-start.15 = (f32[64,1024]{1,0:T(8,128)}, f32[64,1024]{1,0:T(8,128)S(1)}, u32[]{:S(2)}, u32[]{:S(2)}) collective-permute-start(f32[64,1024]{1,0:T(8,128)} %get-tuple-element.889), channel_id=1, source_target_pairs={{16,0},{18,2},{20,4},{22,6},{24,8},{26,10},{28,12},{30,14},{17,1},... | collective-permute-start | bytes 786440 | tf_op jit(solution)/shard_map/ppermute | solution.py:17
  134.9 99.2 %copy-start.6 = (f32[1024]{0:T(1024)S(1)}, f32[1024]{0:T(1024)}, u32[]{:S(2)}) copy-start(f32[1024]{0:T(1024)} %param.20) | copy-start | bytes 12292
  134.9 109.8 %copy-start = (f32[16,1024]{1,0:T(8,128)S(1)}, f32[16,1024]{1,0:T(8,128)}, u32[]{:S(2)}) copy-start(f32[16,1024]{1,0:T(8,128)} %param.21) | copy-start | bytes 196612
  151.8 63.0 %collective-permute-start.24 = (f32[16,1024]{1,0:T(8,128)S(1)}, f32[16,1024]{1,0:T(8,128)S(1)}, u32[]{:S(2)}, u32[]{:S(2)}) collective-permute-start(f32[16,1024]{1,0:T(8,128)S(1)} %get-tuple-element.606), channel_id=1, source_target_pairs={{0,2},{2,4},{4,6},{6,8},{8,10},{10,12},{12,14},{14,16},{16,18},{18... | collective-permute-start | bytes 196616 | tf_op jit(solution)/shard_map/ppermute | solution.py:17
  153.1 63.0 %collective-permute-start.25 = (f32[16,1024]{1,0:T(8,128)S(1)}, f32[16,1024]{1,0:T(8,128)S(1)}, u32[]{:S(2)}, u32[]{:S(2)}) collective-permute-start(f32[16,1024]{1,0:T(8,128)S(1)} %get-tuple-element.613), channel_id=1, source_target_pairs={{0,4},{2,6},{4,8},{6,10},{8,12},{10,14},{12,16},{14,18},{16,20},{1... | collective-permute-start | bytes 196616 | tf_op jit(solution)/shard_map/ppermute | solution.py:17
  192.2 27.1 %collective-permute-start.26 = (f32[16,1024]{1,0:T(8,128)S(1)}, f32[16,1024]{1,0:T(8,128)S(1)}, u32[]{:S(2)}, u32[]{:S(2)}) collective-permute-start(f32[16,1024]{1,0:T(8,128)S(1)} %get-tuple-element.612), channel_id=1, source_target_pairs={{0,6},{2,8},{4,10},{6,12},{8,14},{10,16},{12,18},{14,20},{16,22},{... | collective-permute-start | bytes 196616 | tf_op jit(solution)/shard_map/ppermute | solution.py:17
  201.3 4.4 collective-permute-start.16
  203.7 4.9 collective-permute-start.17
  205.7 5.8 %collective-permute-start.18 = (f32[1024]{0:T(1024)S(1)}, f32[1024]{0:T(1024)S(1)}, u32[]{:S(2)}, u32[]{:S(2)}) collective-permute-start(f32[1024]{0:T(1024)S(1)} %bitcast.243), channel_id=1, source_target_pairs={{0,6},{2,8},{4,10},{6,12},{8,14},{10,16},{12,18},{14,20},{16,22},{... | collective-permute-start | bytes 12296 | tf_op jit(solution)/shard_map/ppermute | solution.py:17
  208.7 11.9 %collective-permute-start.27 = (f32[16,1024]{1,0:T(8,128)S(1)}, f32[16,1024]{1,0:T(8,128)S(1)}, u32[]{:S(2)}, u32[]{:S(2)}) collective-permute-start(f32[16,1024]{1,0:T(8,128)S(1)} %get-tuple-element.611), channel_id=1, source_target_pairs={{0,8},{2,10},{4,12},{6,14},{8,16},{10,18},{12,20},{14,22},{16,24},... | collective-permute-start | bytes 196616 | tf_op jit(solution)/shard_map/ppermute | solution.py:17
  211.5 10.4 %collective-permute-start.28 = (f32[16,1024]{1,0:T(8,128)S(1)}, f32[16,1024]{1,0:T(8,128)S(1)}, u32[]{:S(2)}, u32[]{:S(2)}) collective-permute-start(f32[16,1024]{1,0:T(8,128)S(1)} %get-tuple-element.610), channel_id=1, source_target_pairs={{0,10},{2,12},{4,14},{6,16},{8,18},{10,20},{12,22},{14,24},{16,26}... | collective-permute-start | bytes 196616 | tf_op jit(solution)/shard_map/ppermute | solution.py:17
  214.8 8.4 %collective-permute-start.29 = (f32[16,1024]{1,0:T(8,128)S(1)}, f32[16,1024]{1,0:T(8,128)S(1)}, u32[]{:S(2)}, u32[]{:S(2)}) collective-permute-start(f32[16,1024]{1,0:T(8,128)S(1)} %get-tuple-element.609), channel_id=1, source_target_pairs={{0,12},{2,14},{4,16},{6,18},{8,20},{10,22},{12,24},{14,26},{16,28}... | collective-permute-start | bytes 196616 | tf_op jit(solution)/shard_map/ppermute | solution.py:17
  216.1 8.4 %collective-permute-start.30 = (f32[16,1024]{1,0:T(8,128)S(1)}, f32[16,1024]{1,0:T(8,128)S(1)}, u32[]{:S(2)}, u32[]{:S(2)}) collective-permute-start(f32[16,1024]{1,0:T(8,128)S(1)} %get-tuple-element.608), channel_id=1, source_target_pairs={{0,14},{2,16},{4,18},{6,20},{8,22},{10,24},{12,26},{14,28},{16,30}... | collective-permute-start | bytes 196616 | tf_op jit(solution)/shard_map/ppermute | solution.py:17
  219.3 9.7 %collective-permute-start.31 = (f32[16,1024]{1,0:T(8,128)S(1)}, f32[16,1024]{1,0:T(8,128)S(1)}, u32[]{:S(2)}, u32[]{:S(2)}) collective-permute-start(f32[16,1024]{1,0:T(8,128)S(1)} %get-tuple-element.607), channel_id=1, source_target_pairs={{0,16},{2,18},{4,20},{6,22},{8,24},{10,26},{12,28},{14,30},{1,17},... | collective-permute-start | bytes 196616 | tf_op jit(solution)/shard_map/ppermute | solution.py:17
  220.6 10.4 %collective-permute-start.19 = (f32[1024]{0:T(1024)S(1)}, f32[1024]{0:T(1024)S(1)}, u32[]{:S(2)}, u32[]{:S(2)}) collective-permute-start(f32[1024]{0:T(1024)S(1)} %bitcast.241), channel_id=1, source_target_pairs={{0,8},{2,10},{4,12},{6,14},{8,16},{10,18},{12,20},{14,22},{16,24},... | collective-permute-start | bytes 12296 | tf_op jit(solution)/shard_map/ppermute | solution.py:17
  221.9 9.1 %collective-permute-start.20 = (f32[1024]{0:T(1024)S(1)}, f32[1024]{0:T(1024)S(1)}, u32[]{:S(2)}, u32[]{:S(2)}) collective-permute-start(f32[1024]{0:T(1024)S(1)} %bitcast.239), channel_id=1, source_target_pairs={{0,10},{2,12},{4,14},{6,16},{8,18},{10,20},{12,22},{14,24},{16,26}... | collective-permute-start | bytes 12296 | tf_op jit(solution)/shard_map/ppermute | solution.py:17
  223.2 7.8 %collective-permute-start.21 = (f32[1024]{0:T(1024)S(1)}, f32[1024]{0:T(1024)S(1)}, u32[]{:S(2)}, u32[]{:S(2)}) collective-permute-start(f32[1024]{0:T(1024)S(1)} %bitcast.237), channel_id=1, source_target_pairs={{0,12},{2,14},{4,16},{6,18},{8,20},{10,22},{12,24},{14,26},{16,28}... | collective-permute-start | bytes 12296 | tf_op jit(solution)/shard_map/ppermute | solution.py:17
  224.6 6.5 %collective-permute-start.22 = (f32[1024]{0:T(1024)S(1)}, f32[1024]{0:T(1024)S(1)}, u32[]{:S(2)}, u32[]{:S(2)}) collective-permute-start(f32[1024]{0:T(1024)S(1)} %bitcast.235), channel_id=1, source_target_pairs={{0,14},{2,16},{4,18},{6,20},{8,22},{10,24},{12,26},{14,28},{16,30}... | collective-permute-start | bytes 12296 | tf_op jit(solution)/shard_map/ppermute | solution.py:17
  229.0 2.6 collective-permute-start.23
  231.0 227.0 %all-reduce.6.cloned.1.call-start = ((), (), s32[]{:S(2)}) async-start(), calls=%async_computation.1 | async-start | bytes 131072 | tf_op jit(solution)/shard_map/psum | solution.py:110
  326.2 6.9 %collective-permute-start.32 = (bf16[16,1024]{1,0:T(8,128)(2,1)S(1)}, bf16[16,1024]{1,0:T(8,128)(2,1)S(1)}, u32[]{:S(2)}, u32[]{:S(2)}) collective-permute-start(bf16[16,1024]{1,0:T(8,128)(2,1)S(1)} %convert.173), channel_id=1, source_target_pairs={{2,0},{4,2},{6,4},{8,6},{10,8},{12,10},{14,12},{16,14},{18,16},{20... | collective-permute-start | bytes 98312 | tf_op jit(solution)/shard_map/ppermute | solution.py:17
  327.5 7.9 %collective-permute-start.33 = (bf16[16,1024]{1,0:T(8,128)(2,1)S(1)}, bf16[16,1024]{1,0:T(8,128)(2,1)S(1)}, u32[]{:S(2)}, u32[]{:S(2)}) collective-permute-start(bf16[16,1024]{1,0:T(8,128)(2,1)S(1)} %convert.173), channel_id=1, source_target_pairs={{4,0},{6,2},{8,4},{10,6},{12,8},{14,10},{16,12},{18,14},{20,16},{2... | collective-permute-start | bytes 98312 | tf_op jit(solution)/shard_map/ppermute | solution.py:17
  328.8 8.5 %collective-permute-start.34 = (bf16[16,1024]{1,0:T(8,128)(2,1)S(1)}, bf16[16,1024]{1,0:T(8,128)(2,1)S(1)}, u32[]{:S(2)}, u32[]{:S(2)}) collective-permute-start(bf16[16,1024]{1,0:T(8,128)(2,1)S(1)} %convert.173), channel_id=1, source_target_pairs={{6,0},{8,2},{10,4},{12,6},{14,8},{16,10},{18,12},{20,14},{22,16},{... | collective-permute-start | bytes 98312 | tf_op jit(solution)/shard_map/ppermute | solution.py:17
  330.1 10.6 %collective-permute-start.35 = (bf16[16,1024]{1,0:T(8,128)(2,1)S(1)}, bf16[16,1024]{1,0:T(8,128)(2,1)S(1)}, u32[]{:S(2)}, u32[]{:S(2)}) collective-permute-start(bf16[16,1024]{1,0:T(8,128)(2,1)S(1)} %convert.173), channel_id=1, source_target_pairs={{8,0},{10,2},{12,4},{14,6},{16,8},{18,10},{20,12},{22,14},{24,16},... | collective-permute-start | bytes 98312 | tf_op jit(solution)/shard_map/ppermute | solution.py:17
  331.4 12.1 %collective-permute-start.36 = (bf16[16,1024]{1,0:T(8,128)(2,1)S(1)}, bf16[16,1024]{1,0:T(8,128)(2,1)S(1)}, u32[]{:S(2)}, u32[]{:S(2)}) collective-permute-start(bf16[16,1024]{1,0:T(8,128)(2,1)S(1)} %convert.173), channel_id=1, source_target_pairs={{10,0},{12,2},{14,4},{16,6},{18,8},{20,10},{22,12},{24,14},{26,16}... | collective-permute-start | bytes 98312 | tf_op jit(solution)/shard_map/ppermute | solution.py:17
  333.1 11.9 %collective-permute-start.37 = (bf16[16,1024]{1,0:T(8,128)(2,1)S(1)}, bf16[16,1024]{1,0:T(8,128)(2,1)S(1)}, u32[]{:S(2)}, u32[]{:S(2)}) collective-permute-start(bf16[16,1024]{1,0:T(8,128)(2,1)S(1)} %convert.173), channel_id=1, source_target_pairs={{12,0},{14,2},{16,4},{18,6},{20,8},{22,10},{24,12},{26,14},{28,16}... | collective-permute-start | bytes 98312 | tf_op jit(solution)/shard_map/ppermute | solution.py:17
  335.4 13.9 %collective-permute-start.38 = (bf16[16,1024]{1,0:T(8,128)(2,1)S(1)}, bf16[16,1024]{1,0:T(8,128)(2,1)S(1)}, u32[]{:S(2)}, u32[]{:S(2)}) collective-permute-start(bf16[16,1024]{1,0:T(8,128)(2,1)S(1)} %convert.173), channel_id=1, source_target_pairs={{14,0},{16,2},{18,4},{20,6},{22,8},{24,10},{26,12},{28,14},{30,16}... | collective-permute-start | bytes 98312 | tf_op jit(solution)/shard_map/ppermute | solution.py:17
  337.3 12.4 %collective-permute-start.39 = (bf16[16,1024]{1,0:T(8,128)(2,1)S(1)}, bf16[16,1024]{1,0:T(8,128)(2,1)S(1)}, u32[]{:S(2)}, u32[]{:S(2)}) collective-permute-start(bf16[16,1024]{1,0:T(8,128)(2,1)S(1)} %get-tuple-element.592), channel_id=1, source_target_pairs={{16,0},{18,2},{20,4},{22,6},{24,8},{26,10},{28,12},{30,14},{17,1},... | collective-permute-start | bytes 98312 | tf_op jit(solution)/shard_map/ppermute | solution.py:17
  363.5 137.5 %copy-start.1 = (f32[16,1024]{1,0:T(8,128)S(1)}, f32[16,1024]{1,0:T(8,128)}, u32[]{:S(2)}) copy-start(f32[16,1024]{1,0:T(8,128)} %all-reduce.4.cloned.1.call-done) | copy-start | bytes 196612
  363.5 64.6 %collective-permute-start.48 = (f32[16,1024]{1,0:T(8,128)S(1)}, f32[16,1024]{1,0:T(8,128)S(1)}, u32[]{:S(2)}, u32[]{:S(2)}) collective-permute-start(f32[16,1024]{1,0:T(8,128)S(1)} %get-tuple-element.598), channel_id=1, source_target_pairs={{0,2},{2,4},{4,6},{6,8},{8,10},{10,12},{12,14},{14,16},{16,18},{18... | collective-permute-start | bytes 196616 | tf_op jit(solution)/shard_map/ppermute | solution.py:17
  366.3 63.1 %collective-permute-start.49 = (f32[16,1024]{1,0:T(8,128)S(1)}, f32[16,1024]{1,0:T(8,128)S(1)}, u32[]{:S(2)}, u32[]{:S(2)}) collective-permute-start(f32[16,1024]{1,0:T(8,128)S(1)} %get-tuple-element.605), channel_id=1, source_target_pairs={{0,4},{2,6},{4,8},{6,10},{8,12},{10,14},{12,16},{14,18},{16,20},{1... | collective-permute-start | bytes 196616 | tf_op jit(solution)/shard_map/ppermute | solution.py:17
  409.1 23.5 %collective-permute-start.50 = (f32[16,1024]{1,0:T(8,128)S(1)}, f32[16,1024]{1,0:T(8,128)S(1)}, u32[]{:S(2)}, u32[]{:S(2)}) collective-permute-start(f32[16,1024]{1,0:T(8,128)S(1)} %get-tuple-element.604), channel_id=1, source_target_pairs={{0,6},{2,8},{4,10},{6,12},{8,14},{10,16},{12,18},{14,20},{16,22},{... | collective-permute-start | bytes 196616 | tf_op jit(solution)/shard_map/ppermute | solution.py:17
  414.6 4.4 collective-permute-start.40
  417.1 4.9 collective-permute-start.41
  419.0 5.8 %collective-permute-start.42 = (f32[1024]{0:T(1024)S(1)}, f32[1024]{0:T(1024)S(1)}, u32[]{:S(2)}, u32[]{:S(2)}) collective-permute-start(f32[1024]{0:T(1024)S(1)} %bitcast.244), channel_id=1, source_target_pairs={{0,6},{2,8},{4,10},{6,12},{8,14},{10,16},{12,18},{14,20},{16,22},{... | collective-permute-start | bytes 12296 | tf_op jit(solution)/shard_map/ppermute | solution.py:17
  422.0 11.9 %collective-permute-start.51 = (f32[16,1024]{1,0:T(8,128)S(1)}, f32[16,1024]{1,0:T(8,128)S(1)}, u32[]{:S(2)}, u32[]{:S(2)}) collective-permute-start(f32[16,1024]{1,0:T(8,128)S(1)} %get-tuple-element.603), channel_id=1, source_target_pairs={{0,8},{2,10},{4,12},{6,14},{8,16},{10,18},{12,20},{14,22},{16,24},... | collective-permute-start | bytes 196616 | tf_op jit(solution)/shard_map/ppermute | solution.py:17
  424.9 10.4 %collective-permute-start.52 = (f32[16,1024]{1,0:T(8,128)S(1)}, f32[16,1024]{1,0:T(8,128)S(1)}, u32[]{:S(2)}, u32[]{:S(2)}) collective-permute-start(f32[16,1024]{1,0:T(8,128)S(1)} %get-tuple-element.602), channel_id=1, source_target_pairs={{0,10},{2,12},{4,14},{6,16},{8,18},{10,20},{12,22},{14,24},{16,26}... | collective-permute-start | bytes 196616 | tf_op jit(solution)/shard_map/ppermute | solution.py:17
  428.1 8.4 %collective-permute-start.53 = (f32[16,1024]{1,0:T(8,128)S(1)}, f32[16,1024]{1,0:T(8,128)S(1)}, u32[]{:S(2)}, u32[]{:S(2)}) collective-permute-start(f32[16,1024]{1,0:T(8,128)S(1)} %get-tuple-element.601), channel_id=1, source_target_pairs={{0,12},{2,14},{4,16},{6,18},{8,20},{10,22},{12,24},{14,26},{16,28}... | collective-permute-start | bytes 196616 | tf_op jit(solution)/shard_map/ppermute | solution.py:17
  429.4 8.4 %collective-permute-start.54 = (f32[16,1024]{1,0:T(8,128)S(1)}, f32[16,1024]{1,0:T(8,128)S(1)}, u32[]{:S(2)}, u32[]{:S(2)}) collective-permute-start(f32[16,1024]{1,0:T(8,128)S(1)} %get-tuple-element.600), channel_id=1, source_target_pairs={{0,14},{2,16},{4,18},{6,20},{8,22},{10,24},{12,26},{14,28},{16,30}... | collective-permute-start | bytes 196616 | tf_op jit(solution)/shard_map/ppermute | solution.py:17
  432.6 9.7 %collective-permute-start.55 = (f32[16,1024]{1,0:T(8,128)S(1)}, f32[16,1024]{1,0:T(8,128)S(1)}, u32[]{:S(2)}, u32[]{:S(2)}) collective-permute-start(f32[16,1024]{1,0:T(8,128)S(1)} %get-tuple-element.599), channel_id=1, source_target_pairs={{0,16},{2,18},{4,20},{6,22},{8,24},{10,26},{12,28},{14,30},{1,17},... | collective-permute-start | bytes 196616 | tf_op jit(solution)/shard_map/ppermute | solution.py:17
  433.9 10.4 %collective-permute-start.43 = (f32[1024]{0:T(1024)S(1)}, f32[1024]{0:T(1024)S(1)}, u32[]{:S(2)}, u32[]{:S(2)}) collective-permute-start(f32[1024]{0:T(1024)S(1)} %bitcast.242), channel_id=1, source_target_pairs={{0,8},{2,10},{4,12},{6,14},{8,16},{10,18},{12,20},{14,22},{16,24},... | collective-permute-start | bytes 12296 | tf_op jit(solution)/shard_map/ppermute | solution.py:17
  435.2 9.1 %collective-permute-start.44 = (f32[1024]{0:T(1024)S(1)}, f32[1024]{0:T(1024)S(1)}, u32[]{:S(2)}, u32[]{:S(2)}) collective-permute-start(f32[1024]{0:T(1024)S(1)} %bitcast.240), channel_id=1, source_target_pairs={{0,10},{2,12},{4,14},{6,16},{8,18},{10,20},{12,22},{14,24},{16,26}... | collective-permute-start | bytes 12296 | tf_op jit(solution)/shard_map/ppermute | solution.py:17
  436.6 7.8 %collective-permute-start.45 = (f32[1024]{0:T(1024)S(1)}, f32[1024]{0:T(1024)S(1)}, u32[]{:S(2)}, u32[]{:S(2)}) collective-permute-start(f32[1024]{0:T(1024)S(1)} %bitcast.238), channel_id=1, source_target_pairs={{0,12},{2,14},{4,16},{6,18},{8,20},{10,22},{12,24},{14,26},{16,28}... | collective-permute-start | bytes 12296 | tf_op jit(solution)/shard_map/ppermute | solution.py:17
  437.9 6.5 %collective-permute-start.46 = (f32[1024]{0:T(1024)S(1)}, f32[1024]{0:T(1024)S(1)}, u32[]{:S(2)}, u32[]{:S(2)}) collective-permute-start(f32[1024]{0:T(1024)S(1)} %bitcast.236), channel_id=1, source_target_pairs={{0,14},{2,16},{4,18},{6,20},{8,22},{10,24},{12,26},{14,28},{16,30}... | collective-permute-start | bytes 12296 | tf_op jit(solution)/shard_map/ppermute | solution.py:17
  442.3 2.6 collective-permute-start.47
  (2 other events, 1.4 us)
Sparse Core Ops, SparseCore 0:
  231.1 13.5 all-reduce.3
  444.4 13.5 all-reduce.5
where the time goes:
time: 513 us; the launch traced here: 509 us
  starting transfers between devices  189 us (37%)
  waiting for transfers between devices  127 us (25%)
  blocking collectives  125 us (24%)
  matrix products  25.8 us (5%)
  between operations  15.8 us (3%)
  other arithmetic  14.6 us (3%)
  local copies, waits for them, and re-layouts  9.3 us (2%)
    ppermute x56, starting transfers between devices, from_behind(): lax.ppermute(value, axis, [(source, source + steps) for source in range(i...  189 us
    ppermute x56, waiting for transfers between devices, from_behind(): lax.ppermute(value, axis, [(source, source + steps) for source in range(i...  105 us
    psum x2, blocking collectives, squares(): return lax.psum(jnp.sum(residual * residual, axis=1), 'blk')  78.5 us
    psum x1, blocking collectives, body(): step_size = norm_now / lax.psum(jnp.sum(direction * applied, axis=1), 'blk')  42 us
    psum x2, waiting for transfers between devices, body(): own_prod, own_deg = lax.psum((own_prod, own_deg), 'rep')  21.3 us
    dot_general x3, matrix products, kernel_tile(): lax.dot_general(rows_z, cols_z, (((0,), (0,)), ((), ())), precision=exact...  19.6 us
  transfers between devices with their start and end apart: 58, of which 22 were waited for; matrix products, arithmetic and copies ran while one was open for 2% of the time, Pallas kernels for 0%

commit v1 on v0

v1 whole, which is shorter than its diff:
```python
import functools

import jax
import jax.numpy as jnp
from jax import lax
from jax.experimental import pallas as pl
from jax.experimental.pallas import tpu as pltpu
from jax.sharding import PartitionSpec as P

W = 8
SLOTS = W // 2
ROWS = 256
SUB = 16
DEPTH = 512
MESH = pl.DeviceIdType.MESH
f32 = jnp.float32
bf16 = jnp.bfloat16


def split3(value):
    hi = value.astype(bf16).astype(f32)
    rest = value - hi
    mid = rest.astype(bf16).astype(f32)
    return hi, mid, rest - mid


def lanes(value):
    total = value[:, 0:128]
    for at in range(128, value.shape[1], 128):
        total = total + value[:, at : at + 128]
    return total


def kernel(
    n, points, scale, noise, target, listed, sol, res,
    z, zp, left, right, sq, tiles, diag, rowacc, total, image, resid, low,
    vp1, vp2, out1, in1, out2, in2, half1, half2, mine, sums,
    zs, zr, v1s, v1r, v2s, v2r, r1s, r1r, r2s, r2r, hs, hr, ss, sr,
):
    blk = lax.axis_index("blk")
    core = lax.axis_index("rep")
    feats, size = points.shape
    cols = target.shape[0]
    half = size // 2

    def offset(k):
        return 1 + 2 * k + core

    def at(block):
        return {"blk": block, "rep": core}

    barrier = pltpu.get_barrier_semaphore()

    @pl.loop(0, n)
    def _(b):
        @pl.when(b != blk)
        def _():
            pl.semaphore_signal(barrier, inc=1, device_id=at(b), device_id_type=MESH)

    pl.semaphore_signal(
        barrier, inc=1, device_id={"blk": blk, "rep": 1 - core}, device_id_type=MESH
    )
    scaled = points[...] / scale[...]
    z[...] = scaled
    low[0] = target[...].astype(bf16)
    pl.semaphore_wait(barrier, n)

    def copy(src, dst, send, recv, block):
        return pltpu.make_async_remote_copy(
            src_ref=src, dst_ref=dst, send_sem=send, recv_sem=recv,
            device_id=at(block), device_id_type=MESH,
        )

    def z_copy(k):
        return copy(z, zp.at[k], zs.at[k], zr.at[k], blk - offset(k))

    def v1_copy(k):
        return copy(low.at[0], vp1.at[k], v1s.at[k], v1r.at[k], blk - offset(k))

    def v2_copy(k):
        return copy(low.at[1], vp2.at[k], v2s.at[k], v2r.at[k], blk - offset(k))

    def ret1_copy(k):
        return copy(out1.at[k], in1.at[k], r1s.at[k], r1r.at[k], blk + offset(k))

    def ret2_copy(k):
        return copy(out2.at[k], in2.at[k], r2s.at[k], r2r.at[k], blk + offset(k))

    def below(k):
        return blk - offset(k) >= 0

    def above(k):
        return blk + offset(k) < n

    for k in range(SLOTS):
        @pl.when(below(k))
        def _(k=k):
            z_copy(k).start()
            v1_copy(k).start()

    def norm_rows(value, first):
        n1, n2, n3 = split3(jnp.sum(value * value, axis=0, keepdims=True))
        i = lax.broadcasted_iota(jnp.int32, (16, size), 0)
        ones = jnp.where((i >= 3 - first) & (i < 6 - first), 1.0, 0.0)
        return jnp.where(
            i == first, n1, jnp.where(i == first + 1, n2, jnp.where(i == first + 2, n3, ones))
        )

    def fill_right(value):
        hi, mid, lo = split3(value)
        for j, part in enumerate((hi, mid, hi, mid, lo, hi)):
            right[j * feats : (j + 1) * feats, :] = part.astype(bf16)
        right[6 * feats : 6 * feats + 16, :] = norm_rows(value, 3).astype(bf16)

    right[6 * feats + 16 :, :] = jnp.zeros((DEPTH - 6 * feats - 16, size), bf16)
    hi, mid, lo = split3(-2.0 * scaled)
    hi2 = jnp.concatenate([hi, hi], axis=0)
    mid2 = jnp.concatenate([mid, mid], axis=0)
    hilo = jnp.concatenate([hi, lo], axis=0)
    tail = jnp.concatenate(
        [norm_rows(scaled, 0), jnp.zeros((112, size), f32)], axis=0
    )
    for j, part in enumerate((hi2, mid2, hilo, tail)):
        left[:, j * 128 : (j + 1) * 128] = part.T.astype(bf16)
    fill_right(scaled)

    def chunk(row, store, weight, with_rows, colacc):
        sq[...] = jnp.dot(
            left[pl.ds(row, ROWS), :], right[...], preferred_element_type=f32
        )
        for sub in range(0, ROWS, SUB):
            square = jnp.maximum(sq[sub : sub + SUB, :], 1e-24)
            radius = square * lax.rsqrt(square)
            margin = jnp.maximum(1.0 - radius, 0.0)
            margin = margin * margin
            value = margin * margin * (radius * (4.0 * weight) + weight)
            store(sub, value.astype(bf16))
            for g in range(0, SUB, 8):
                colacc = colacc + value[g : g + 8, :]
            if with_rows:
                rowacc[pl.ds(pl.multiple_of(row + sub, 8), SUB), :] += lanes(value)
        return colacc

    rowacc[...] = jnp.zeros_like(rowacc)
    inv = 1.0 / size

    def diag_chunk(j, colacc):
        def store(sub, value):
            diag[pl.ds(pl.multiple_of(j * ROWS + sub, 16), SUB), :] = value

        row = pl.multiple_of(core * half + j * ROWS, ROWS)
        return chunk(row, store, inv, False, colacc)

    colacc = lax.fori_loop(0, half // ROWS, diag_chunk, jnp.zeros((8, size), f32))
    own_cols = pl.ds(pl.multiple_of(core * half, 128), half)
    total[0:cols, :] = jnp.dot(low[0, :, own_cols], diag[...], preferred_element_type=f32)
    total[cols:, :] = jnp.zeros((8, size), f32)
    total[cols : cols + 1, :] = jnp.sum(colacc, axis=0, keepdims=True)

    def back(value, tile):
        return lax.dot_general(
            value, tile, (((1,), (1,)), ((), ())), preferred_element_type=f32
        )

    @pl.loop(0, SLOTS)
    def _(k):
        @pl.when(above(k))
        def _():
            z_copy(k).wait_recv()
            v1_copy(k).wait_recv()
            fill_right(zp[k])
            weight = listed[0, offset(k) - 1] * inv

            def step(j, colacc):
                def store(sub, value):
                    tiles[k, pl.ds(pl.multiple_of(j * ROWS + sub, 16), SUB), :] = value

                return chunk(pl.multiple_of(j * ROWS, ROWS), store, weight, True, colacc)

            colacc = lax.fori_loop(0, size // ROWS, step, jnp.zeros((8, size), f32))
            tile = tiles.at[k]
            out1[k, 0:cols, :] = jnp.dot(low[0], tile[...], preferred_element_type=f32)
            out1[k, cols:, :] = jnp.broadcast_to(
                jnp.sum(colacc, axis=0, keepdims=True), (8, size)
            )
            ret1_copy(k).start()
            total[0:cols, :] += back(vp1[k], tile[...])

    total[cols : cols + 1, :] += jnp.sum(rowacc[...].T, axis=0, keepdims=True)

    def collect(inbox, get, dst, send, recv):
        for k in range(SLOTS):
            @pl.when(below(k))
            def _(k=k):
                get(k).wait_recv()
                total[0 : inbox.shape[1], :] += inbox[k]

        src = total.at[pl.ds(0, inbox.shape[1])]
        swap = pltpu.make_async_remote_copy(
            src_ref=src, dst_ref=dst, send_sem=send, recv_sem=recv,
            device_id={"blk": blk, "rep": 1 - core}, device_id_type=MESH,
        )
        swap.start()
        swap.wait()

    def sum_start(which, values):
        for j, value in enumerate(values):
            mine[which, j * cols : (j + 1) * cols, :] = lanes(value)
        sums[which, pl.ds(blk, 1)] = mine[pl.ds(which, 1)]

        @pl.loop(0, n)
        def _(b):
            @pl.when(b != blk)
            def _():
                copy(mine.at[which], sums.at[which, blk], ss.at[which, b], sr.at[which, blk], b).start()

    def sum_end(which):
        @pl.loop(0, n)
        def _(b):
            @pl.when(b != blk)
            def _():
                one = copy(mine.at[which], sums.at[which, b], ss.at[which, b], sr.at[which, b], b)
                one.wait_recv()
                one.wait_send()

        return jnp.sum(jnp.sum(sums[which], axis=0), axis=1, keepdims=True)

    collect(in1, ret1_copy, half1, hs.at[0], hr.at[0])
    total[...] += half1[...]
    direction = target[...]
    diagonal = total[cols : cols + 1, :] + noise[...]
    image[...] = diagonal * direction + total[0:cols, :]
    sum_start(0, (direction * direction, direction * image[...]))
    both = sum_end(0)
    norm_now = both[0:cols]
    step1 = norm_now / both[cols : 2 * cols]
    residual = target[...] - step1 * image[...]
    resid[...] = residual
    low[1] = residual.astype(bf16)
    for k in range(SLOTS):
        @pl.when(below(k))
        def _(k=k):
            v2_copy(k).start()
    sum_start(1, (residual * residual, jnp.zeros_like(residual)))

    total[0:cols, :] = jnp.dot(low[1, :, own_cols], diag[...], preferred_element_type=f32)

    @pl.loop(0, SLOTS)
    def _(k):
        @pl.when(above(k))
        def _():
            tile = tiles.at[k]
            out2[k] = jnp.dot(low[1], tile[...], preferred_element_type=f32)
            ret2_copy(k).start()
            v2_copy(k).wait_recv()
            total[0:cols, :] += back(vp2[k], tile[...])

    norm_next = sum_end(1)[0:cols]
    collect(in2, ret2_copy, half2, hs.at[1], hr.at[1])
    beta = norm_next / norm_now
    direction = resid[...] + beta * target[...]
    image2 = (
        diagonal * resid[...] + (total[0:cols, :] + half2[...]) + beta * image[...]
    )
    dots = direction * image2
    sum_start(2, (dots, jnp.zeros_like(dots)))
    step2 = norm_next / sum_end(2)[0:cols]
    sol[...] = step1 * target[...] + step2 * direction
    res[...] = resid[...] - step2 * image2

    for k in range(SLOTS):
        @pl.when(below(k))
        def _(k=k):
            z_copy(k).wait_send()
            v1_copy(k).wait_send()
            v2_copy(k).wait_send()

        @pl.when(above(k))
        def _(k=k):
            ret1_copy(k).wait_send()
            ret2_copy(k).wait_send()


def body(n, points, lengthscale, noise, target, pair_offset, pair_count):
    feats, size = points.shape
    cols = target.shape[0]
    live = jnp.arange(W)[None, :] < pair_count[:, None]
    match = pair_offset[0][None, :] == jnp.arange(1, W + 1)[:, None]
    listed = jnp.any(match & live, axis=1).astype(f32)[None, :]
    vmem = pl.BlockSpec(memory_space=pltpu.VMEM)
    dma = pltpu.SemaphoreType.DMA
    V = pltpu.VMEM
    return pl.pallas_call(
        functools.partial(kernel, n),
        out_shape=[jax.ShapeDtypeStruct((cols, size), f32)] * 2,
        in_specs=[vmem, vmem, vmem, vmem, pl.BlockSpec(memory_space=pltpu.SMEM)],
        out_specs=[vmem, vmem],
        scratch_shapes=[
            V((feats, size), f32),
            V((SLOTS, feats, size), f32),
            V((size, DEPTH), bf16),
            V((DEPTH, size), bf16),
            V((ROWS, size), f32),
            V((SLOTS, size, size), bf16),
            V((size // 2, size), bf16),
            V((size, 128), f32),
            V((cols + 8, size), f32),
            V((cols, size), f32),
            V((cols, size), f32),
            V((2, cols, size), bf16),
            V((SLOTS, cols, size), bf16),
            V((SLOTS, cols, size), bf16),
            V((SLOTS, cols + 8, size), f32),
            V((SLOTS, cols + 8, size), f32),
            V((SLOTS, cols, size), f32),
            V((SLOTS, cols, size), f32),
            V((cols + 8, size), f32),
            V((cols, size), f32),
            V((3, 2 * cols, 128), f32),
            V((3, n, 2 * cols, 128), f32),
        ]
        + [dma((SLOTS,))] * 10
        + [dma((2,))] * 2
        + [dma((3, n))] * 2,
        compiler_params=pltpu.CompilerParams(
            collective_id=0, has_side_effects=True, vmem_limit_bytes=48 * 1024 * 1024
        ),
    )(points, lengthscale[:, None], noise[None, :], target, listed)


def solution(mesh):
    n = mesh.shape["blk"]
    placed = (P(None, "blk"), P(), P("blk"), P(None, "blk"), P("blk", None), P("blk"))
    return jax.shard_map(
        functools.partial(body, n),
        mesh=mesh,
        in_specs=placed,
        out_specs=(P(None, "blk"), P(None, "blk")),
        check_vma=False,
    )
```

time: 513 us -> 94.9 us (0.18)
  starting transfers between devices: 189 us -> 0 us
  waiting for transfers between devices: 127 us -> 0 us
  blocking collectives: 125 us -> 0 us
  Pallas kernels: 0 us -> 88.2 us
  matrix products: 25.8 us -> 0 us
  between operations: 15.8 us -> 1.32 us
  other arithmetic: 14.6 us -> 0.2 us
    ppermute x56 -> x0, starting transfers between devices: 189 us -> none  [from_behind(): lax.ppermute(value, axis, [(source, source + steps) for source in range(i...]
    psum x5 -> x0, blocking collectives: 125 us -> none  [the longest x2 78.5 us: squares(): return lax.psum(jnp.sum(residual * residual, axis=1), 'blk')]
    ppermute x56 -> x0, waiting for transfers between devices: 105 us -> none  [from_behind(): lax.ppermute(value, axis, [(source, source + steps) for source in range(i...]
    pallas_call x0 -> x1, Pallas kernels: none -> 88.2 us  [body(): pl.pallas_call(functools.partial(kernel, n), out_shape=[jax.ShapeDtypeStr...]
    dot_general x9 -> x0, matrix products: 25.8 us -> none  [the longest x3 19.6 us: kernel_tile(): lax.dot_general(rows_z, cols_z, (((0,), (0,)), ((), ())), precision=exact...]
    psum x2 -> x0, waiting for transfers between devices: 21.3 us -> none  [body(): own_prod, own_deg = lax.psum((own_prod, own_deg), 'rep')]
    reduce_sum x7 -> x0, other arithmetic: 5.72 us -> none  [the longest x2 1.93 us: body(): step_size = norm_now / lax.psum(jnp.sum(direction * applied, axis=1), 'blk')]
  transfers between devices with their start and end apart: 58 -> 0, of which waited for: 22 -> 0; matrix products, arithmetic and copies ran while one was open for 2% -> 0% of each run, Pallas kernels for 0% -> 0%
where the time goes in v1:
time: 94.9 us; the launch traced here: 94.7 us
  Pallas kernels  88.2 us (93%)
  local copies, waits for them, and re-layouts  5.02 us (5%)
  between operations  1.32 us (1%)
    pallas_call x1, Pallas kernels, body(): pl.pallas_call(functools.partial(kernel, n), out_shape=[jax.ShapeDtypeStr...  88.2 us
    unnamed x12, local copies, waits for them, and re-layouts  4.92 us

profile of v1, /device:TPU:0, one launch (start us, length us, event | category | flops | bytes accessed | tf_op | source)
XLA Modules:
  0.0 94.7 jit_solution(1320320131841047770)
XLA Ops:
  1.3 0.0 copy-start.4
  1.3 0.6 copy-done.4
  1.9 0.2 and_reduce_fusion
  2.1 0.0 copy-start.3
  2.1 0.6 copy-done.3
  2.8 0.0 copy-start.2
  2.8 0.1 copy.9.scale
  2.9 0.6 copy-done.2
  3.5 0.0 copy-start
  3.5 0.9 %copy-done = f32[64,1024]{1,0:T(8,128)S(1)} copy-done((f32[64,1024]{1,0:T(8,128)S(1)}, f32[64,1024]{1,0:T(8,128)}, u32[]{:S(2)}) %copy-start) | copy-done | bytes 262168
  4.4 0.0 copy-start.1
  4.4 0.8 copy-done.1
  5.3 88.2 %shard_map.77 = (f32[16,1024]{1,0:T(8,128)S(1)}, f32[16,1024]{1,0:T(8,128)S(1)}) custom-call(f32[64,1024]{1,0:T(8,128)S(1)} %copy-done, f32[64,1]{1,0:T(8,128)S(1)} %copy.9.scale, f32[1,1024]{1,0:T(1,128)S(1)} %bitcast.7, f32[16,1024]{1,0:T(8,128)S(1)} %copy-done.1, f32[1,8]{1,0:T(1,128)S(1)} %convert_bitcast_fusion.listed), custom_call_target="tpu_custom_call" | custom-call | tf_op jit(solution)/shard_map/pallas_call | solution.py:293
  93.4 0.6 copy.13
  94.1 0.6 copy.14
  (3 shorter events, 0.0 us)
Async XLA Ops:
  1.3 0.7 copy-start.4
  2.1 0.7 copy-start.3
  2.8 0.7 copy-start.2
  3.5 0.9 %copy-start = (f32[64,1024]{1,0:T(8,128)S(1)}, f32[64,1024]{1,0:T(8,128)}, u32[]{:S(2)}) copy-start(f32[64,1024]{1,0:T(8,128)} %points.1) | copy-start | bytes 786436
  4.4 0.8 copy-start.1

commit v2 on v1

--- a/solution.py
+++ b/solution.py
@@ -35,7 +35,7 @@
     n, points, scale, noise, target, listed, sol, res,
     z, zp, left, right, sq, tiles, diag, rowacc, total, image, resid, low,
     vp1, vp2, out1, in1, out2, in2, half1, half2, mine, sums,
-    zs, zr, v1s, v1r, v2s, v2r, r1s, r1r, r2s, r2r, hs, hr, ss, sr,
+    outd, ind, zs, zr, ds, dr, v1s, v1r, v2s, v2r, r1s, r1r, r2s, r2r, hs, hr, ss, sr,
 ):
     blk = lax.axis_index("blk")
     core = lax.axis_index("rep")
@@ -49,6 +49,11 @@
     def at(block):
         return {"blk": block, "rep": core}
 
+    first = lax.div(blk, 4) * 4
+
+    def mate(m):
+        return first + lax.rem(blk - first + m, 4)
+
     barrier = pltpu.get_barrier_semaphore()
 
     @pl.loop(0, n)
@@ -57,13 +62,14 @@
         def _():
             pl.semaphore_signal(barrier, inc=1, device_id=at(b), device_id_type=MESH)
 
-    pl.semaphore_signal(
-        barrier, inc=1, device_id={"blk": blk, "rep": 1 - core}, device_id_type=MESH
-    )
+    for m in range(4):
+        pl.semaphore_signal(
+            barrier, inc=1, device_id={"blk": mate(m), "rep": 1 - core}, device_id_type=MESH
+        )
     scaled = points[...] / scale[...]
     z[...] = scaled
     low[0] = target[...].astype(bf16)
-    pl.semaphore_wait(barrier, n)
+    pl.semaphore_wait(barrier, n + 3)
 
     def copy(src, dst, send, recv, block):
         return pltpu.make_async_remote_copy(
@@ -71,8 +77,42 @@
             device_id=at(block), device_id_type=MESH,
         )
 
-    def z_copy(k):
-        return copy(z, zp.at[k], zs.at[k], zr.at[k], blk - offset(k))
+    def z_send(src, shift, block, sem):
+        slot, owner = lax.div(shift - 1, 2), lax.rem(shift - 1, 2)
+        return pltpu.make_async_remote_copy(
+            src_ref=src, dst_ref=zp.at[slot], send_sem=zs.at[sem], recv_sem=zr.at[slot],
+            device_id={"blk": block, "rep": owner}, device_id_type=MESH,
+        )
+
+    def z_wait(k):
+        copy(z, zp.at[k], zs.at[0], zr.at[k], blk).wait_recv()
+
+    def own_sends(act):
+        for m in (1, 2, 3):
+            @pl.when((core == 0) & (mate(m) < blk))
+            def _(m=m):
+                act(z_send(z, blk - mate(m), mate(m), m - 1))
+
+        @pl.when((core == 1) & (blk >= 4))
+        def _():
+            act(z_send(z, 4, blk - 4, 0))
+
+    def relay_near(act):
+        @pl.when(blk >= 4)
+        def _():
+            act(z_send(zp.at[1], 8, blk - 4, 1))
+
+        for m in (1, 2, 3):
+            act(z_send(zp.at[1], blk + 4 - mate(m), mate(m), 1 + m))
+
+    def relay_far(act):
+        for m in (1, 2, 3):
+            @pl.when(mate(m) > blk)
+            def _(m=m):
+                act(z_send(zp.at[3], blk + 8 - mate(m), mate(m), 4 + m))
+
+    def deg_copy(k):
+        return copy(outd.at[k], ind.at[k], ds.at[k], dr.at[k], blk + offset(k))
 
     def v1_copy(k):
         return copy(low.at[0], vp1.at[k], v1s.at[k], v1r.at[k], blk - offset(k))
@@ -91,11 +131,12 @@
 
     def above(k):
         return blk + offset(k) < n
+
+    own_sends(lambda one: one.start())
 
     for k in range(SLOTS):
         @pl.when(below(k))
         def _(k=k):
-            z_copy(k).start()
             v1_copy(k).start()
 
     def norm_rows(value, first):
@@ -162,11 +203,26 @@
             value, tile, (((1,), (1,)), ((), ())), preferred_element_type=f32
         )
 
+    @pl.when((core == 1) & (blk + 4 < n))
+    def _():
+        z_wait(1)
+        relay_near(lambda one: one.start())
+
+    @pl.when((core == 1) & (blk + 8 < n))
+    def _():
+        z_wait(3)
+        relay_far(lambda one: one.start())
+
     @pl.loop(0, SLOTS)
-    def _(k):
+    def _(step_k):
+        k = lax.rem(step_k + core, SLOTS)
+
         @pl.when(above(k))
         def _():
-            z_copy(k).wait_recv()
+            @pl.when((core == 0) | (lax.rem(k, 2) == 0))
+            def _():
+                z_wait(k)
+
             v1_copy(k).wait_recv()
             fill_right(zp[k])
             weight = listed[0, offset(k) - 1] * inv
@@ -179,10 +235,9 @@
 
             colacc = lax.fori_loop(0, size // ROWS, step, jnp.zeros((8, size), f32))
             tile = tiles.at[k]
-            out1[k, 0:cols, :] = jnp.dot(low[0], tile[...], preferred_element_type=f32)
-            out1[k, cols:, :] = jnp.broadcast_to(
-                jnp.sum(colacc, axis=0, keepdims=True), (8, size)
-            )
+            outd[k] = jnp.sum(colacc, axis=0, keepdims=True)
+            deg_copy(k).start()
+            out1[k] = jnp.dot(low[0], tile[...], preferred_element_type=f32)
             ret1_copy(k).start()
             total[0:cols, :] += back(vp1[k], tile[...])
 
@@ -193,9 +248,9 @@
             @pl.when(below(k))
             def _(k=k):
                 get(k).wait_recv()
-                total[0 : inbox.shape[1], :] += inbox[k]
-
-        src = total.at[pl.ds(0, inbox.shape[1])]
+                total[0:cols, :] += inbox[k]
+
+        src = total.at[pl.ds(0, dst.shape[0])]
         swap = pltpu.make_async_remote_copy(
             src_ref=src, dst_ref=dst, send_sem=send, recv_sem=recv,
             device_id={"blk": blk, "rep": 1 - core}, device_id_type=MESH,
@@ -203,9 +258,18 @@
         swap.start()
         swap.wait()
 
+    def spot(j):
+        row = lax.broadcasted_iota(jnp.int32, (cols, 128), 0)
+        return lax.broadcasted_iota(jnp.int32, (cols, 128), 1) == row + j * cols
+
     def sum_start(which, values):
-        for j, value in enumerate(values):
-            mine[which, j * cols : (j + 1) * cols, :] = lanes(value)
+        mine[which] = sum(
+            jnp.sum(
+                jnp.where(spot(j), jnp.sum(value, axis=1, keepdims=True), 0.0),
+                axis=0, keepdims=True,
+            )
+            for j, value in enumerate(values)
+        )
         sums[which, pl.ds(blk, 1)] = mine[pl.ds(which, 1)]
 
         @pl.loop(0, n)
@@ -214,7 +278,7 @@
             def _():
                 copy(mine.at[which], sums.at[which, blk], ss.at[which, b], sr.at[which, blk], b).start()
 
-    def sum_end(which):
+    def sum_end(which, count):
         @pl.loop(0, n)
         def _(b):
             @pl.when(b != blk)
@@ -223,7 +287,16 @@
                 one.wait_recv()
                 one.wait_send()
 
-        return jnp.sum(jnp.sum(sums[which], axis=0), axis=1, keepdims=True)
+        row = jnp.sum(sums[which], axis=0)
+        return [
+            jnp.sum(jnp.where(spot(j), row, 0.0), axis=1, keepdims=True) for j in range(count)
+        ]
+
+    for k in range(SLOTS):
+        @pl.when(below(k))
+        def _(k=k):
+            deg_copy(k).wait_recv()
+            total[cols : cols + 1, :] += ind[k]
 
     collect(in1, ret1_copy, half1, hs.at[0], hr.at[0])
     total[...] += half1[...]
@@ -231,9 +304,8 @@
     diagonal = total[cols : cols + 1, :] + noise[...]
     image[...] = diagonal * direction + total[0:cols, :]
     sum_start(0, (direction * direction, direction * image[...]))
-    both = sum_end(0)
-    norm_now = both[0:cols]
-    step1 = norm_now / both[cols : 2 * cols]
+    norm_now, curve = sum_end(0, 2)
+    step1 = norm_now / curve
     residual = target[...] - step1 * image[...]
     resid[...] = residual
     low[1] = residual.astype(bf16)
@@ -241,7 +313,7 @@
         @pl.when(below(k))
         def _(k=k):
             v2_copy(k).start()
-    sum_start(1, (residual * residual, jnp.zeros_like(residual)))
+    sum_start(1, (residual * residual,))
 
     total[0:cols, :] = jnp.dot(low[1, :, own_cols], diag[...], preferred_element_type=f32)
 
@@ -255,29 +327,38 @@
             v2_copy(k).wait_recv()
             total[0:cols, :] += back(vp2[k], tile[...])
 
-    norm_next = sum_end(1)[0:cols]
+    norm_next = sum_end(1, 1)[0]
     collect(in2, ret2_copy, half2, hs.at[1], hr.at[1])
     beta = norm_next / norm_now
     direction = resid[...] + beta * target[...]
     image2 = (
         diagonal * resid[...] + (total[0:cols, :] + half2[...]) + beta * image[...]
     )
-    dots = direction * image2
-    sum_start(2, (dots, jnp.zeros_like(dots)))
-    step2 = norm_next / sum_end(2)[0:cols]
+    sum_start(2, (direction * image2,))
+    step2 = norm_next / sum_end(2, 1)[0]
     sol[...] = step1 * target[...] + step2 * direction
     res[...] = resid[...] - step2 * image2
+
+    own_sends(lambda one: one.wait_send())
+
+    @pl.when((core == 1) & (blk + 4 < n))
+    def _():
+        relay_near(lambda one: one.wait_send())
+
+    @pl.when((core == 1) & (blk + 8 < n))
+    def _():
+        relay_far(lambda one: one.wait_send())
 
     for k in range(SLOTS):
         @pl.when(below(k))
         def _(k=k):
-            z_copy(k).wait_send()
             v1_copy(k).wait_send()
             v2_copy(k).wait_send()
 
         @pl.when(above(k))
         def _(k=k):
             ret1_copy(k).wait_send()
+            deg_copy(k).wait_send()
             ret2_copy(k).wait_send()
 
 
@@ -310,15 +391,18 @@
             V((2, cols, size), bf16),
             V((SLOTS, cols, size), bf16),
             V((SLOTS, cols, size), bf16),
-            V((SLOTS, cols + 8, size), f32),
-            V((SLOTS, cols + 8, size), f32),
+            V((SLOTS, cols, size), f32),
+            V((SLOTS, cols, size), f32),
             V((SLOTS, cols, size), f32),
             V((SLOTS, cols, size), f32),
             V((cols + 8, size), f32),
             V((cols, size), f32),
-            V((3, 2 * cols, 128), f32),
-            V((3, n, 2 * cols, 128), f32),
+            V((3, 1, 128), f32),
+            V((3, n, 1, 128), f32),
+            V((SLOTS, 1, size), f32),
+            V((SLOTS, 1, size), f32),
         ]
+        + [dma((W,)), dma((SLOTS,))]
         + [dma((SLOTS,))] * 10
         + [dma((2,))] * 2
         + [dma((3, n))] * 2,

time: 94.9 us -> 72.7 us (0.77)
  Pallas kernels: 88.2 us -> 65.9 us
    pallas_call x1, Pallas kernels: 88.2 us -> 65.9 us  [body(): pl.pallas_call(functools.partial(kernel, n), out_shape=[jax.ShapeDtypeStr...]
where the time goes in v2:
time: 72.7 us; the launch traced here: 72.5 us
  Pallas kernels  65.9 us (91%)
  local copies, waits for them, and re-layouts  5.02 us (7%)
  between operations  1.32 us (2%)
    pallas_call x1, Pallas kernels, body(): pl.pallas_call(functools.partial(kernel, n), out_shape=[jax.ShapeDtypeStr...  65.9 us
    unnamed x12, local copies, waits for them, and re-layouts  4.92 us

profile of v2, /device:TPU:0, one launch (start us, length us, event | category | flops | bytes accessed | tf_op | source)
XLA Modules:
  0.0 72.5 jit_solution(16668057560020341567)
XLA Ops:
  1.3 0.0 copy-start.4
  1.3 0.6 copy-done.4
  1.9 0.2 and_reduce_fusion
  2.1 0.0 copy-start.3
  2.1 0.6 copy-done.3
  2.8 0.0 copy-start.2
  2.8 0.1 copy.9.scale
  2.9 0.6 copy-done.2
  3.5 0.0 copy-start
  3.5 0.9 %copy-done = f32[64,1024]{1,0:T(8,128)S(1)} copy-done((f32[64,1024]{1,0:T(8,128)S(1)}, f32[64,1024]{1,0:T(8,128)}, u32[]{:S(2)}) %copy-start) | copy-done | bytes 262168
  4.4 0.0 copy-start.1
  4.4 0.8 %copy-done.1 = f32[16,1024]{1,0:T(8,128)S(1)} copy-done((f32[16,1024]{1,0:T(8,128)S(1)}, f32[16,1024]{1,0:T(8,128)}, u32[]{:S(2)}) %copy-start.1) | copy-done | bytes 65560
  5.3 65.9 %shard_map.77 = (f32[16,1024]{1,0:T(8,128)S(1)}, f32[16,1024]{1,0:T(8,128)S(1)}) custom-call(f32[64,1024]{1,0:T(8,128)S(1)} %copy-done, f32[64,1]{1,0:T(8,128)S(1)} %copy.9.scale, f32[1,1024]{1,0:T(1,128)S(1)} %bitcast.7, f32[16,1024]{1,0:T(8,128)S(1)} %copy-done.1, f32[1,8]{1,0:T(1,128)S(1)} %convert_bitcast_fusion.listed), custom_call_target="tpu_custom_call" | custom-call | tf_op jit(solution)/shard_map/pallas_call | solution.py:374
  71.2 0.6 copy.13
  71.8 0.6 copy.14
  (3 shorter events, 0.0 us)
Async XLA Ops:
  1.3 0.7 copy-start.4
  2.1 0.7 copy-start.3
  2.8 0.7 copy-start.2
  3.5 0.9 %copy-start = (f32[64,1024]{1,0:T(8,128)S(1)}, f32[64,1024]{1,0:T(8,128)}, u32[]{:S(2)}) copy-start(f32[64,1024]{1,0:T(8,128)} %points.1) | copy-start | bytes 786436
  4.4 0.8 %copy-start.1 = (f32[16,1024]{1,0:T(8,128)S(1)}, f32[16,1024]{1,0:T(8,128)}, u32[]{:S(2)}) copy-start(f32[16,1024]{1,0:T(8,128)} %target.1) | copy-start | bytes 196612

commit v3 on v2

--- a/solution.py
+++ b/solution.py
@@ -35,7 +35,7 @@
     n, points, scale, noise, target, listed, sol, res,
     z, zp, left, right, sq, tiles, diag, rowacc, total, image, resid, low,
     vp1, vp2, out1, in1, out2, in2, half1, half2, mine, sums,
-    outd, ind, zs, zr, ds, dr, v1s, v1r, v2s, v2r, r1s, r1r, r2s, r2r, hs, hr, ss, sr,
+    acc, outd, ind, zs, zr, ds, dr, v1s, v1r, v2s, v2r, r1s, r1r, r2s, r2r, hs, hr, ss, sr,
 ):
     blk = lax.axis_index("blk")
     core = lax.axis_index("rep")
@@ -198,10 +198,13 @@
     total[cols:, :] = jnp.zeros((8, size), f32)
     total[cols : cols + 1, :] = jnp.sum(colacc, axis=0, keepdims=True)
 
+    acc[...] = jnp.zeros_like(acc)
+
     def back(value, tile):
-        return lax.dot_general(
-            value, tile, (((1,), (1,)), ((), ())), preferred_element_type=f32
-        )
+        wide = jnp.concatenate(
+            [value.astype(f32), jnp.zeros((128 - cols, size), f32)], axis=0
+        )
+        acc[...] += jnp.dot(tile, wide.T.astype(bf16), preferred_element_type=f32)
 
     @pl.when((core == 1) & (blk + 4 < n))
     def _():
@@ -239,8 +242,10 @@
             deg_copy(k).start()
             out1[k] = jnp.dot(low[0], tile[...], preferred_element_type=f32)
             ret1_copy(k).start()
-            total[0:cols, :] += back(vp1[k], tile[...])
-
+            back(vp1[k], tile[...])
+
+    total[0:cols, :] += acc[...].T[0:cols, :]
+    acc[...] = jnp.zeros_like(acc)
     total[cols : cols + 1, :] += jnp.sum(rowacc[...].T, axis=0, keepdims=True)
 
     def collect(inbox, get, dst, send, recv):
@@ -321,11 +326,17 @@
     def _(k):
         @pl.when(above(k))
         def _():
-            tile = tiles.at[k]
-            out2[k] = jnp.dot(low[1], tile[...], preferred_element_type=f32)
+            out2[k] = jnp.dot(low[1], tiles[k], preferred_element_type=f32)
             ret2_copy(k).start()
+
+    @pl.loop(0, SLOTS)
+    def _(k):
+        @pl.when(above(k))
+        def _():
             v2_copy(k).wait_recv()
-            total[0:cols, :] += back(vp2[k], tile[...])
+            back(vp2[k], tiles[k])
+
+    total[0:cols, :] += acc[...].T[0:cols, :]
 
     norm_next = sum_end(1, 1)[0]
     collect(in2, ret2_copy, half2, hs.at[1], hr.at[1])
@@ -399,6 +410,7 @@
             V((cols, size), f32),
             V((3, 1, 128), f32),
             V((3, n, 1, 128), f32),
+            V((size, 128), f32),
             V((SLOTS, 1, size), f32),
             V((SLOTS, 1, size), f32),
         ]

time: 72.7 us -> 71.2 us (0.979)
  Pallas kernels: 65.9 us -> 64.4 us
    pallas_call x1, Pallas kernels: 65.9 us -> 64.4 us  [body(): pl.pallas_call(functools.partial(kernel, n), out_shape=[jax.ShapeDtypeStr...]
where the time goes in v3:
time: 71.2 us; the launch traced here: 70.9 us
  Pallas kernels  64.4 us (90%)
  local copies, waits for them, and re-layouts  5.02 us (7%)
  between operations  1.32 us (2%)
    pallas_call x1, Pallas kernels, body(): pl.pallas_call(functools.partial(kernel, n), out_shape=[jax.ShapeDtypeStr...  64.4 us
    unnamed x12, local copies, waits for them, and re-layouts  4.92 us

profile of v3, /device:TPU:0, one launch (start us, length us, event | category | flops | bytes accessed | tf_op | source)
XLA Modules:
  0.0 70.9 jit_solution(12126513365264349159)
XLA Ops:
  1.3 0.0 copy-start.4
  1.3 0.6 copy-done.4
  1.9 0.2 and_reduce_fusion
  2.1 0.0 copy-start.3
  2.1 0.6 copy-done.3
  2.8 0.0 copy-start.2
  2.8 0.1 copy.9.scale
  2.9 0.6 copy-done.2
  3.5 0.0 copy-start
  3.5 0.9 %copy-done = f32[64,1024]{1,0:T(8,128)S(1)} copy-done((f32[64,1024]{1,0:T(8,128)S(1)}, f32[64,1024]{1,0:T(8,128)}, u32[]{:S(2)}) %copy-start) | copy-done | bytes 262168
  4.4 0.0 copy-start.1
  4.4 0.8 %copy-done.1 = f32[16,1024]{1,0:T(8,128)S(1)} copy-done((f32[16,1024]{1,0:T(8,128)S(1)}, f32[16,1024]{1,0:T(8,128)}, u32[]{:S(2)}) %copy-start.1) | copy-done | bytes 65560
  5.3 64.4 %shard_map.77 = (f32[16,1024]{1,0:T(8,128)S(1)}, f32[16,1024]{1,0:T(8,128)S(1)}) custom-call(f32[64,1024]{1,0:T(8,128)S(1)} %copy-done, f32[64,1]{1,0:T(8,128)S(1)} %copy.9.scale, f32[1,1024]{1,0:T(1,128)S(1)} %bitcast.7, f32[16,1024]{1,0:T(8,128)S(1)} %copy-done.1, f32[1,8]{1,0:T(1,128)S(1)} %convert_bitcast_fusion.listed), custom_call_target="tpu_custom_call" | custom-call | tf_op jit(solution)/shard_map/pallas_call | solution.py:385
  69.7 0.6 copy.13
  70.3 0.6 copy.14
  (3 shorter events, 0.0 us)
Async XLA Ops:
  1.3 0.7 copy-start.4
  2.1 0.7 copy-start.3
  2.8 0.7 copy-start.2
  3.5 0.9 %copy-start = (f32[64,1024]{1,0:T(8,128)S(1)}, f32[64,1024]{1,0:T(8,128)}, u32[]{:S(2)}) copy-start(f32[64,1024]{1,0:T(8,128)} %points.1) | copy-start | bytes 786436
  4.4 0.8 %copy-start.1 = (f32[16,1024]{1,0:T(8,128)S(1)}, f32[16,1024]{1,0:T(8,128)}, u32[]{:S(2)}) copy-start(f32[16,1024]{1,0:T(8,128)} %target.1) | copy-start | bytes 196612

commit v4 on v3

--- a/solution.py
+++ b/solution.py
@@ -192,6 +192,11 @@
         row = pl.multiple_of(core * half + j * ROWS, ROWS)
         return chunk(row, store, inv, False, colacc)
 
+    @pl.when((core == 1) & (blk + 4 < n))
+    def _():
+        z_wait(1)
+        relay_near(lambda one: one.start())
+
     colacc = lax.fori_loop(0, half // ROWS, diag_chunk, jnp.zeros((8, size), f32))
     own_cols = pl.ds(pl.multiple_of(core * half, 128), half)
     total[0:cols, :] = jnp.dot(low[0, :, own_cols], diag[...], preferred_element_type=f32)
@@ -205,11 +210,6 @@
             [value.astype(f32), jnp.zeros((128 - cols, size), f32)], axis=0
         )
         acc[...] += jnp.dot(tile, wide.T.astype(bf16), preferred_element_type=f32)
-
-    @pl.when((core == 1) & (blk + 4 < n))
-    def _():
-        z_wait(1)
-        relay_near(lambda one: one.start())
 
     @pl.when((core == 1) & (blk + 8 < n))
     def _():

time: 71.2 us -> 71.2 us (level)
  no operation moved by 1% of the time
where the time goes in v4:
time: 71.2 us; the launch traced here: 70.9 us
  Pallas kernels  64.4 us (90%)
  local copies, waits for them, and re-layouts  5.02 us (7%)
  between operations  1.32 us (2%)
    pallas_call x1, Pallas kernels, body(): pl.pallas_call(functools.partial(kernel, n), out_shape=[jax.ShapeDtypeStr...  64.4 us
    unnamed x12, local copies, waits for them, and re-layouts  4.92 us

profile of v4, /device:TPU:0, one launch (start us, length us, event | category | flops | bytes accessed | tf_op | source)
XLA Modules:
  0.0 70.9 jit_solution(1865853675845764292)
XLA Ops:
  1.3 0.0 copy-start.4
  1.3 0.6 copy-done.4
  1.9 0.2 and_reduce_fusion
  2.1 0.0 copy-start.3
  2.1 0.6 copy-done.3
  2.8 0.0 copy-start.2
  2.8 0.1 copy.9.scale
  2.9 0.6 copy-done.2
  3.5 0.0 copy-start
  3.5 0.9 %copy-done = f32[64,1024]{1,0:T(8,128)S(1)} copy-done((f32[64,1024]{1,0:T(8,128)S(1)}, f32[64,1024]{1,0:T(8,128)}, u32[]{:S(2)}) %copy-start) | copy-done | bytes 262168
  4.4 0.0 copy-start.1
  4.4 0.8 %copy-done.1 = f32[16,1024]{1,0:T(8,128)S(1)} copy-done((f32[16,1024]{1,0:T(8,128)S(1)}, f32[16,1024]{1,0:T(8,128)}, u32[]{:S(2)}) %copy-start.1) | copy-done | bytes 65560
  5.3 64.4 %shard_map.77 = (f32[16,1024]{1,0:T(8,128)S(1)}, f32[16,1024]{1,0:T(8,128)S(1)}) custom-call(f32[64,1024]{1,0:T(8,128)S(1)} %copy-done, f32[64,1]{1,0:T(8,128)S(1)} %copy.9.scale, f32[1,1024]{1,0:T(1,128)S(1)} %bitcast.7, f32[16,1024]{1,0:T(8,128)S(1)} %copy-done.1, f32[1,8]{1,0:T(1,128)S(1)} %convert_bitcast_fusion.listed), custom_call_target="tpu_custom_call" | custom-call | tf_op jit(solution)/shard_map/pallas_call | solution.py:385
  69.7 0.6 copy.13
  70.3 0.6 copy.14
  (3 shorter events, 0.0 us)
Async XLA Ops:
  1.3 0.7 copy-start.4
  2.1 0.7 copy-start.3
  2.8 0.7 copy-start.2
  3.5 0.9 %copy-start = (f32[64,1024]{1,0:T(8,128)S(1)}, f32[64,1024]{1,0:T(8,128)}, u32[]{:S(2)}) copy-start(f32[64,1024]{1,0:T(8,128)} %points.1) | copy-start | bytes 786436
  4.4 0.8 %copy-start.1 = (f32[16,1024]{1,0:T(8,128)S(1)}, f32[16,1024]{1,0:T(8,128)}, u32[]{:S(2)}) copy-start(f32[16,1024]{1,0:T(8,128)} %target.1) | copy-start | bytes 196612

commit v5 on v4

--- a/solution.py
+++ b/solution.py
@@ -32,7 +32,8 @@
 
 
 def kernel(
-    n, points, scale, noise, target, listed, sol, res,
+    n, points_hbm, scale_hbm, noise_hbm, target_hbm, offsets, count, sol, res,
+    points, scale, noise, target, loads,
     z, zp, left, right, sq, tiles, diag, rowacc, total, image, resid, low,
     vp1, vp2, out1, in1, out2, in2, half1, half2, mine, sums,
     acc, outd, ind, zs, zr, ds, dr, v1s, v1r, v2s, v2r, r1s, r1r, r2s, r2r, hs, hr, ss, sr,
@@ -54,6 +55,15 @@
     def mate(m):
         return first + lax.rem(blk - first + m, 4)
 
+    fetches = [
+        pltpu.make_async_copy(src, dst, loads.at[j])
+        for j, (src, dst) in enumerate(
+            ((points_hbm, points), (scale_hbm, scale), (target_hbm, target), (noise_hbm, noise))
+        )
+    ]
+    for fetch in fetches:
+        fetch.start()
+
     barrier = pltpu.get_barrier_semaphore()
 
     @pl.loop(0, n)
@@ -66,6 +76,8 @@
         pl.semaphore_signal(
             barrier, inc=1, device_id={"blk": mate(m), "rep": 1 - core}, device_id_type=MESH
         )
+    for fetch in fetches:
+        fetch.wait()
     scaled = points[...] / scale[...]
     z[...] = scaled
     low[0] = target[...].astype(bf16)
@@ -228,7 +240,10 @@
 
             v1_copy(k).wait_recv()
             fill_right(zp[k])
-            weight = listed[0, offset(k) - 1] * inv
+            weight = sum(
+                jnp.where((offsets[0, s] == offset(k)) & (s < count[0]), inv, 0.0)
+                for s in range(W)
+            )
 
             def step(j, colacc):
                 def store(sub, value):
@@ -376,18 +391,21 @@
 def body(n, points, lengthscale, noise, target, pair_offset, pair_count):
     feats, size = points.shape
     cols = target.shape[0]
-    live = jnp.arange(W)[None, :] < pair_count[:, None]
-    match = pair_offset[0][None, :] == jnp.arange(1, W + 1)[:, None]
-    listed = jnp.any(match & live, axis=1).astype(f32)[None, :]
     vmem = pl.BlockSpec(memory_space=pltpu.VMEM)
     dma = pltpu.SemaphoreType.DMA
     V = pltpu.VMEM
     return pl.pallas_call(
         functools.partial(kernel, n),
         out_shape=[jax.ShapeDtypeStruct((cols, size), f32)] * 2,
-        in_specs=[vmem, vmem, vmem, vmem, pl.BlockSpec(memory_space=pltpu.SMEM)],
+        in_specs=[pl.BlockSpec(memory_space=pltpu.HBM)] * 4
+        + [pl.BlockSpec(memory_space=pltpu.SMEM)] * 2,
         out_specs=[vmem, vmem],
         scratch_shapes=[
+            V((feats, size), f32),
+            V((feats, 1), f32),
+            V((1, size), f32),
+            V((cols, size), f32),
+            dma((4,)),
             V((feats, size), f32),
             V((SLOTS, feats, size), f32),
             V((size, DEPTH), bf16),
@@ -419,9 +437,9 @@
         + [dma((2,))] * 2
         + [dma((3, n))] * 2,
         compiler_params=pltpu.CompilerParams(
-            collective_id=0, has_side_effects=True, vmem_limit_bytes=48 * 1024 * 1024
+            collective_id=0, has_side_effects=True, vmem_limit_bytes=63 * 1024 * 1024
         ),
-    )(points, lengthscale[:, None], noise[None, :], target, listed)
+    )(points, lengthscale[:, None], noise[None, :], target, pair_offset, pair_count)
 
 
 def solution(mesh):

time: 71.2 us -> 70.6 us (level)
  local copies, waits for them, and re-layouts: 5.02 us -> 3.5 us
  Pallas kernels: 64.4 us -> 65.6 us
    unnamed x12 -> x6, local copies, waits for them, and re-layouts: 4.92 us -> 2.79 us
    pallas_call x1, Pallas kernels: 64.4 us -> 65.6 us  [body(): pl.pallas_call(functools.partial(kernel, n), out_shape=[jax.ShapeDtypeStr...]
where the time goes in v5:
time: 70.6 us; the launch traced here: 70.4 us
  Pallas kernels  65.6 us (93%)
  local copies, waits for them, and re-layouts  3.5 us (5%)
  between operations  1.3 us (2%)
    pallas_call x1, Pallas kernels, body(): pl.pallas_call(functools.partial(kernel, n), out_shape=[jax.ShapeDtypeStr...  65.6 us
    unnamed x6, local copies, waits for them, and re-layouts  2.79 us

profile of v5, /device:TPU:0, one launch (start us, length us, event | category | flops | bytes accessed | tf_op | source)
XLA Modules:
  0.0 70.4 jit_solution(2958842115353898944)
XLA Ops:
  1.3 0.0 copy-start.1
  1.3 0.6 copy-done.1
  1.9 0.7 %copy.8.scale_hbm = f32[64,1]{1,0:T(8,128)} copy(f32[64,1]{0,1:T(1,128)S(1)} %bitcast.3) | data formatting | bytes 512 | tf_op jit(solution)/shard_map/broadcast_in_dim | solution.py:442
  2.6 65.6 %shard_map.77 = (f32[16,1024]{1,0:T(8,128)}, f32[16,1024]{1,0:T(8,128)}) custom-call(f32[64,1024]{1,0:T(8,128)} %points_hbm.1, f32[64,1]{1,0:T(8,128)} %copy.8.scale_hbm, f32[1,1024]{1,0:T(1,128)} %bitcast.2, f32[16,1024]{1,0:T(8,128)} %target_hbm.1, s32[1,8]{1,0:T(1,128)} %offsets.1, s32[1]{0:T(128)S(6)} %copy.11.count), custom_call_target="tpu_custom_call" | custom-call | tf_op jit(solution)/shard_map/pallas_call | solution.py:397
  68.2 0.0 copy-start
  68.2 1.5 %copy.12 = f32[16,1024]{1,0:T(8,128)} copy(f32[16,1024]{1,0:T(8,128)} %get-tuple-element.4) | data formatting | bytes 131072
  69.7 0.0 copy-done
  69.7 0.6 copy.13
Async XLA Ops:
  1.3 0.7 copy-start.1
  68.2 1.5 %copy-start = (f32[16,1024]{1,0:T(8,128)S(1)}, f32[16,1024]{1,0:T(8,128)}, u32[]{:S(2)}) copy-start(f32[16,1024]{1,0:T(8,128)} %get-tuple-element.5) | copy-start | bytes 196612
